TPU v7x, 128 devices: a whole 4x4x4 slice. The times are simulated.
128 devices in a mesh: outer: 4 (over z_lo, core), inner: 32 (over z_hi, y, x).
Axes of the slice: x: 4, y: 4, z: 4 (z_hi: 2, z_lo: 2; z = z_hi * 2 + z_lo), core: 2. Of those that a mesh axis runs over, the one named last changes fastest.
Arguments:
- vertex: float32 [524288, 128], P(('outer', 'inner')), may hold values from -1.75 to 1.75
- context: float32 [262144, 128], P(('outer', 'inner')), may hold values from -1.75 to 1.75
- tile_count: int32 [512], P(('outer', 'inner')), may hold values from 1 to 8, as said below
- tile_vert: int32 [512, 8], P(('outer', 'inner')), may hold values from 0 to 15
- tile_context: int32 [512, 8], P(('outer', 'inner')), may hold values from 0 to 7
- positives: int32 [512, 8, 256], P(('outer', 'inner')), may hold values from 0 to 255
- negatives: int32 [512, 8, 4, 256], P(('outer', 'inner')), may hold values from 0 to 255
Outputs:
- vertex_out: float32 [524288, 128], P(('outer', 'inner'))
- context_out: float32 [262144, 128], P(('outer', 'inner'))
Inputs may be any that keep to these rules, and one draw needn't show every extreme that they name: `tile_count`: every entry is at least 1, and in every tour step some device has all 8 slots live.
All inputs are finite; a program needn't handle non-finite values.
Results may differ from a plain program's by a relative error of at most 0.0003.
Values sent between devices are 32-bit elements; how exact they have to be, the bound alone decides.
No kernel may reach another device: no remote copies, remote signals or barrier semaphores. Data moves between devices by JAX's collectives and lax.ppermute only.
A program may use at most 64 MiB of HBM per device.

v0:
```python
import jax
import jax.numpy as jnp
from jax import lax
from jax.experimental import pallas as pl
from jax.experimental.pallas import tpu as pltpu
from jax.sharding import PartitionSpec as P

TILE = 256
WIDTH = 128
SLOTS = 8
NEG = 4
AXES = ("outer", "inner")
META = 40
SIDE = 48
LISTED = 96
VERT_TILES = 16
CTX_TILES = 8
HALF = 8 * TILE
FIRST_LIMIT = 60 * 1024 * 1024
STEP_LIMIT = 20 * 1024 * 1024

ANY = pl.BlockSpec(memory_space=pl.ANY)
HBM = pl.BlockSpec(memory_space=pltpu.HBM)


def route(groups, members, odd, move):
    pairs = []
    for o in range(odd, groups, 2):
        for i in range(members):
            to = ((o + move[0]) % groups) * members + (i + move[1]) % members
            pairs.append((o * members + i, to))
    return pairs


def wide(rows):
    return jax.ShapeDtypeStruct((rows, WIDTH), jnp.float32)


def vmem(rows):
    return pltpu.VMEM((rows, WIDTH), jnp.float32)


def tile(n):
    return pl.ds(pl.multiple_of(n * TILE, TILE), TILE)


def started(copies):
    for copy in copies:
        copy.start()
    return copies


def waited(copies):
    for copy in copies:
        copy.wait()


def moved(pairs, sems, first=0):
    return started(
        [
            pltpu.make_async_copy(source, to, sems.at[first + n])
            for n, (source, to) in enumerate(pairs)
        ]
    )


def halves(x):
    high = x.astype(jnp.bfloat16)
    return high, (x - high.astype(jnp.float32)).astype(jnp.bfloat16)


def dot(a, b, dims):
    return lax.dot_general(a, b, (dims, ((), ())), preferred_element_type=jnp.float32)


def slot_update(v, c, pos_row, neg_rows, live):
    v_hi, v_lo = halves(v)
    c_hi, c_lo = halves(c)
    c_both = jnp.concatenate([c_hi, c_lo], axis=1)
    v_both = jnp.concatenate([v_hi, v_lo], axis=1)
    scores = dot(
        jnp.concatenate([c_hi, c_lo, c_hi], axis=1),
        jnp.concatenate([v_hi, v_hi, v_lo], axis=1),
        ((1,), (1,)),
    )
    column = lax.broadcasted_iota(jnp.int32, (TILE, TILE), 0)
    at_pos = pos_row == column
    quarter = jnp.where(live, -0.25, 0.0)
    scale = jnp.where(at_pos, quarter, 0.0)
    for row in neg_rows:
        scale = scale + jnp.where(row == column, quarter, 0.0)
    grad = scale * jnp.tanh(0.5 * scores) + (scale + jnp.where(at_pos, -2.0 * quarter, 0.0))
    g_hi, g_lo = halves(grad)
    dc = dot(
        jnp.concatenate([g_hi, g_lo], axis=1),
        jnp.concatenate([v_both, v_both], axis=0),
        ((1,), (0,)),
    )
    dv = dot(
        jnp.concatenate([g_hi, g_lo], axis=0),
        jnp.concatenate([c_both, c_both], axis=0),
        ((0,), (0,)),
    )
    return dv[:, :WIDTH] + dv[:, WIDTH:], dc[:, :WIDTH] + dc[:, WIDTH:]


def choose(chosen, count, here):
    mine = jnp.int32(0)
    for t in range(SLOTS):
        chosen[mine] = t
        mine = mine + ((t < count) & here(t)).astype(jnp.int32)
    return mine


def run_pairs(chosen, mine, one):
    def pair(n, carry):
        results = []
        for at in (2 * n, 2 * n + 1):
            live = at < mine
            results.append(one(chosen[jnp.where(live, at, 0)], live))
        for v_to, vi, dv, c_to, ci, dc in results:
            v_to[tile(vi), :] += dv
            c_to[tile(ci), :] += dc
        return carry

    lax.fori_loop(0, (mine + 1) // 2, pair, 0)


def group_odd():
    return lax.rem(lax.axis_index("outer"), 2)


def first_kernel(steps, *refs):
    vertex, context, count_in, vert_in, ctx_in, pos_in, neg_in, *refs = refs
    low_out, high_out, moved_out, ctx_out, vert_out, own_out, names_out, *refs = refs
    v_old, v_new, c_old, c_new, count, vert, ctx, pos, neg, own, chosen, sems = refs
    heads = moved([(count_in, count), (vert_in, vert), (ctx_in, ctx)], sems)
    lists = moved([(pos_in, pos), (neg_in, neg)], sems, 3)
    loads = moved([(context, c_old), (vertex, v_old)], sems, 5)
    waited(heads)
    mine = choose(chosen, count[0], lambda t: True)
    waited(lists)
    lane = lax.broadcasted_iota(jnp.int32, (8, 128), 1)
    for s in range(1, steps):
        base = LISTED * (s - 1)
        for side in (0, 1):
            lanes = slice(128 * side, 128 * side + 128)
            at = base + SIDE * side
            own[at : at + 8, :] = pos[s, :, lanes].astype(jnp.float32)
            for t in range(SLOTS):
                rows = slice(at + 8 + NEG * t, at + 8 + NEG * t + NEG)
                own[rows, :] = neg[s, t, :, lanes].astype(jnp.float32)
        meta = jnp.where(lane == 16, count[s], 0)
        for t in range(SLOTS):
            meta = jnp.where(lane == t, vert[s, t], meta)
            meta = jnp.where(lane == 8 + t, ctx[s, t], meta)
        meta = meta.astype(jnp.float32)
        own[base + META : base + SIDE, :] = meta
        own[base + SIDE + META : base + LISTED, :] = meta
    waited(loads)

    def fill(n, carry):
        c_new[tile(n), :] = c_old[tile(n), :]
        v_new[tile(2 * n), :] = v_old[tile(2 * n), :]
        v_new[tile(2 * n + 1), :] = v_old[tile(2 * n + 1), :]
        return carry

    lax.fori_loop(0, CTX_TILES, fill, 0)

    def one(t, live):
        vi, ci = vert[0, t], ctx[0, t]
        rows = [neg[0, t, pl.ds(k, 1), :] for k in range(NEG)]
        pos_row = pos[0, pl.ds(t, 1), :]
        dv, dc = slot_update(v_old[tile(vi), :], c_old[tile(ci), :], pos_row, rows, live)
        return v_new, vi, dv, c_new, ci, dc

    run_pairs(chosen, mine, one)
    odd = group_odd()

    @pl.when(odd == 0)
    def even_group():
        stores = [
            (v_new.at[pl.ds(0, HALF)], low_out),
            (v_new.at[pl.ds(HALF, HALF)], high_out),
            (c_new, ctx_out),
            (own, own_out),
        ]
        waited(moved(stores, sems))

    @pl.when(odd == 1)
    def odd_group():
        stores = [
            (c_new, moved_out.at[pl.ds(0, HALF)]),
            (own, moved_out.at[pl.ds(HALF, LISTED * (steps - 1))]),
            (v_new, vert_out),
            (own.at[pl.ds(LISTED * (steps - 2) + META, 8)], names_out),
        ]
        waited(moved(stores, sems))


def first_step(vertex, context, lists):
    steps = lists[0].shape[0]
    listed = LISTED * (steps - 1)

    def kernel(*refs):
        first_kernel(steps, *refs)

    return pl.pallas_call(
        kernel,
        out_shape=[
            wide(HALF),
            wide(HALF),
            wide(HALF + listed),
            wide(HALF),
            wide(2 * HALF),
            wide(listed),
            wide(8),
        ],
        in_specs=[ANY] * 7,
        out_specs=[ANY] * 7,
        scratch_shapes=[
            vmem(2 * HALF),
            vmem(2 * HALF),
            vmem(HALF),
            vmem(HALF),
            pltpu.SMEM((steps,), jnp.int32),
            pltpu.SMEM((steps, SLOTS), jnp.int32),
            pltpu.SMEM((steps, SLOTS), jnp.int32),
            pltpu.VMEM((steps, SLOTS, TILE), jnp.int32),
            pltpu.VMEM((steps, SLOTS, NEG, TILE), jnp.int32),
            vmem(listed),
            pltpu.SMEM((SLOTS + 1,), jnp.int32),
            pltpu.SemaphoreType.DMA((7,)),
        ],
        compiler_params=pltpu.CompilerParams(vmem_limit_bytes=FIRST_LIMIT),
        cost_estimate=pl.CostEstimate(flops=1000, bytes_accessed=1000, transcendentals=0),
    )(vertex, context, *lists)


def head(meta, lane):
    return meta[0, lane].astype(jnp.int32)


def listed_rows(listed, t):
    def row(r):
        both = [listed[pl.ds(r, 1), :], listed[pl.ds(SIDE + r, 1), :]]
        return jnp.concatenate(both, axis=1).astype(jnp.int32)

    return row(t), [row(8 + NEG * t + k) for k in range(NEG)]


def even_kernel(s, half, joined, swaps, n_after, *refs):
    move_in, stay_in, *refs = refs
    total_in = stay_in
    if joined:
        total_in, *refs = refs
    own, *refs = refs
    if swaps:
        give, *refs = refs
    move_out, stay_out, *refs = refs[n_after:]
    m_old, m_new, s_old, s_new, listed, meta, chosen, sems = refs
    if swaps:

        @pl.when(group_odd() == 1)
        def hand_on():
            waited(moved([(give, move_out)], sems))

    @pl.when(group_odd() == 0)
    def work():
        list_in = own.at[pl.ds(LISTED * (s - 1), LISTED)]
        heads = moved([(list_in.at[pl.ds(META, 8)], meta)], sems)
        loads = [
            (list_in, listed),
            (move_in, m_old),
            (stay_in, s_old),
            (move_in, m_new),
            (total_in, s_new),
        ]
        loads = moved(loads, sems, 1)
        waited(heads)
        mine = choose(chosen, head(meta, 16), lambda t: head(meta, t) // 8 == half)
        waited(loads)

        def one(t, live):
            vi, ci = lax.rem(head(meta, t), 8), head(meta, 8 + t)
            rows = listed_rows(listed, t)
            dv, dc = slot_update(m_old[tile(vi), :], s_old[tile(ci), :], *rows, live)
            return m_new, vi, dv, s_new, ci, dc

        run_pairs(chosen, mine, one)
        stores = [(m_new, move_out.at[pl.ds(0, HALF)]), (s_new, stay_out)]
        waited(moved(stores, sems))


def even_step(s, half, moving, staying, total, own, give, after):
    swaps = give is not None
    operands = [moving, staying] + ([] if total is None else [total]) + [own]
    operands += ([give] if swaps else []) + [*after]
    size = give.shape[0] if swaps else HALF

    def kernel(*refs):
        even_kernel(s, half, total is not None, swaps, len(after), *refs)

    return pl.pallas_call(
        kernel,
        out_shape=[wide(size), wide(HALF)],
        in_specs=[ANY] * len(operands),
        out_specs=[ANY, ANY],
        scratch_shapes=[
            vmem(HALF),
            vmem(HALF),
            vmem(HALF),
            vmem(HALF),
            vmem(LISTED),
            pltpu.SMEM((8, 128), jnp.float32),
            pltpu.SMEM((SLOTS + 1,), jnp.int32),
            pltpu.SemaphoreType.DMA((6,)),
        ],
        compiler_params=pltpu.CompilerParams(vmem_limit_bytes=STEP_LIMIT),
        cost_estimate=pl.CostEstimate(flops=1000, bytes_accessed=1000, transcendentals=0),
    )(*operands)


def part_tiles(meta, used, order):
    for n in range(VERT_TILES):
        used[n] = 0
    for t in range(SLOTS):
        at = head(meta, t)
        used[at] = jnp.where(t < head(meta, 16), 1, used[at])
    early, late = jnp.int32(0), jnp.int32(SLOTS)
    for n in range(VERT_TILES):
        soon = (used[n] == 0) & (early < SLOTS)
        order[jnp.where(soon, early, late)] = n
        early = early + soon.astype(jnp.int32)
        late = late + 1 - soon.astype(jnp.int32)


def odd_kernel(left, n_after, *refs):
    move_in, stay_in, *refs = refs
    if left == 1:
        names, *refs = refs
    refs = refs[n_after:]
    move_out, *refs = refs
    if left:
        stay_out, *refs = refs
    if left < 2:
        part_out, *refs = refs
    m_old, m_new, s_old, s_new, listed, metas, chosen, used, order, places, sems = refs

    @pl.when(group_odd() == 1)
    def work():
        meta = metas.at[0]
        split = metas.at[1 if left else 0]
        heads = [(move_in.at[pl.ds(HALF + META, 8)], meta)]
        if left == 1:
            heads.append((names, split))
        heads = moved(heads, sems)
        loads = [
            (move_in.at[pl.ds(HALF, LISTED)], listed),
            (move_in.at[pl.ds(0, HALF)], m_old),
            (stay_in, s_old),
            (move_in.at[pl.ds(0, HALF)], m_new),
            (stay_in, s_new),
        ]
        if left:
            rest = pl.ds(HALF, LISTED * left)
            loads.append((move_in.at[pl.ds(HALF + LISTED, LISTED * left)], move_out.at[rest]))
        loads = moved(loads, sems, 2)
        waited(heads)
        mine = choose(chosen, head(meta, 16), lambda t: True)
        if left < 2:
            part_tiles(split, used, order)
        waited(loads)

        def one(t, live):
            vi, ci = head(meta, t), head(meta, 8 + t)
            rows = listed_rows(listed, t)
            dv, dc = slot_update(s_old[tile(vi), :], m_old[tile(ci), :], *rows, live)
            return s_new, vi, dv, m_new, ci, dc

        run_pairs(chosen, mine, one)
        stores = [(m_new, move_out.at[pl.ds(0, HALF)])]
        if left:
            stores.append((s_new, stay_out))
        if left < 2:
            first = 0 if left else SLOTS
            stores += [
                (s_new.at[tile(order[first + n])], part_out.at[pl.ds(n * TILE, TILE)])
                for n in range(SLOTS)
            ]
        if not left:
            lane = lax.broadcasted_iota(jnp.int32, (8, 128), 1)
            spot = jnp.zeros((8, 128), jnp.int32)
            for n in range(VERT_TILES):
                spot = jnp.where(lane == n, order[n], spot)
            places[...] = spot.astype(jnp.float32)
            stores.append((places, part_out.at[pl.ds(HALF, 8)]))
        waited(moved(stores, sems))


def odd_step(left, moving, staying, names, after):
    operands = [moving, staying] + ([names] if left == 1 else [])
    out_shape = [wide(HALF + LISTED * left)]
    if left:
        out_shape.append(wide(2 * HALF))
    if left < 2:
        out_shape.append(wide(HALF if left else HALF + 8))

    def kernel(*refs):
        odd_kernel(left, len(after), *refs)

    return pl.pallas_call(
        kernel,
        out_shape=out_shape,
        in_specs=[ANY] * (len(operands) + len(after)),
        out_specs=[ANY] * len(out_shape),
        scratch_shapes=[
            vmem(HALF),
            vmem(HALF),
            vmem(2 * HALF),
            vmem(2 * HALF),
            vmem(LISTED),
            pltpu.SMEM((2, 8, 128), jnp.float32),
            pltpu.SMEM((SLOTS + 1,), jnp.int32),
            pltpu.SMEM((VERT_TILES,), jnp.int32),
            pltpu.SMEM((VERT_TILES,), jnp.int32),
            vmem(8),
            pltpu.SemaphoreType.DMA((12,)),
        ],
        compiler_params=pltpu.CompilerParams(vmem_limit_bytes=STEP_LIMIT),
        cost_estimate=pl.CostEstimate(flops=1000, bytes_accessed=1000, transcendentals=0),
    )(*operands, *after)


def finish_kernel(first, second, late, stayed, home, vertex, context, spots, sems):
    odd = group_odd()

    @pl.when(odd == 0)
    def even_group():
        heads = moved([(late.at[pl.ds(HALF, 8)], spots)], sems)
        kept = moved([(stayed, context)], sems, 1)
        waited(heads)
        copies = []
        for n in range(VERT_TILES):
            source = first if n < SLOTS else late
            rows = pl.ds(n % SLOTS * TILE, TILE)
            copies.append((source.at[rows], vertex.at[tile(head(spots, n))]))
        waited(moved(copies, sems, 2))
        waited(kept)

    @pl.when(odd == 1)
    def odd_group():
        copies = [
            (first, vertex.at[pl.ds(0, HALF)]),
            (second, vertex.at[pl.ds(HALF, HALF)]),
            (home, context),
        ]
        waited(moved(copies, sems))


def finish(*operands):
    return pl.pallas_call(
        finish_kernel,
        out_shape=[wide(2 * HALF), wide(HALF)],
        in_specs=[ANY] * 5,
        out_specs=[HBM, HBM],
        scratch_shapes=[
            pltpu.SMEM((8, 128), jnp.float32),
            pltpu.SemaphoreType.DMA((2 + VERT_TILES,)),
        ],
        compiler_params=pltpu.CompilerParams(vmem_limit_bytes=1024 * 1024),
    )(*operands)


def body(vertex, context, *lists):
    groups, members = lax.axis_size("outer"), lax.axis_size("inner")
    steps = lists[0].shape[0]

    def sent(array, odd, move):
        return lax.ppermute(array, AXES, route(groups, members, odd, move))

    low, high, o, c_state, v_state, own, names = first_step(vertex, context, lists)
    names = sent(names, 1, (0, 1 - steps))
    e = [sent(low, 0, (0, 1)), sent(high, 0, (0, 1))]
    o = sent(o, 1, (0, -1))

    def even_half(s, h, total, give=None, *after):
        x, total = even_step(s, h, e[h], c_state, total, own, give, after)
        if s + 1 < steps:
            e[h] = sent(x, 0, (0, 1))
        elif h:
            e[h] = sent(x, 0, (1, 0))
        else:
            swap = route(groups, members, 0, (1, 0)) + route(groups, members, 1, (-1, 0))
            e[h] = lax.ppermute(x, AXES, swap)
        return total

    def odd_whole(s, *after):
        x, *rest = odd_step(steps - 1 - s, o, v_state, names, after)
        return sent(x, 1, (0, -1) if s + 1 < steps else (0, steps - 1)), *rest

    beside = (2, steps - 1)
    total = even_half(1, 0, None)
    c_state = even_half(1, 1, total)
    total = even_half(2, 0, None)
    c_state = even_half(2, 1, total)
    o, v_state = odd_whole(1)
    o, v_state, early = odd_whole(2)
    early = sent(early, 1, beside)
    o, late = odd_whole(3)
    total = even_half(3, 0, None, early, late)
    late = sent(late, 1, (1, steps - 1))
    c_state = even_half(3, 1, total, None, o)
    return tuple(finish(*e, late, c_state, o))


def solution(mesh):
    return jax.shard_map(
        body,
        mesh=mesh,
        in_specs=(
            P(AXES, None),
            P(AXES, None),
            P(AXES),
            P(AXES, None),
            P(AXES, None),
            P(AXES, None, None),
            P(AXES, None, None, None),
        ),
        out_specs=(P(AXES, None), P(AXES, None)),
        check_vma=False,
    )
```

profile of v0, /device:TPU:0, one launch (start us, length us, event | category | flops | bytes accessed | tf_op | source)
XLA Modules:
  0.0 133.6 jit_solution(13852290314336565603)
XLA Ops:
  0.6 5.8 %shard_map.86 = (f32[2048,128]{1,0:T(8,128)}, f32[2048,128]{1,0:T(8,128)}, f32[2336,128]{1,0:T(8,128)}, f32[2048,128]{1,0:T(8,128)}, f32[4096,128]{1,0:T(8,128)}, /*index=5*/f32[288,128]{1,0:T(8,128)}, f32[8,128]{1,0:T(8,128)}) custom-call(f32[4096,128]{1,0:T(8,128)} %refs_0_.1, f32[2048,128]{1,0:T(8,128)} %refs_1_.1, s32[4]{0:T(128)} %refs_2_.1, ...), custom_call_target="tpu_custom_call" | custom-call | flops 1000 | bytes 1000 | tf_op jit(solution)/shard_map/pallas_call | solution.py:208
  6.5 0.7 collective-permute-start.5
  7.2 1.6 %copy-done.2 = f32[4096,128]{1,0:T(8,128)S(1)} copy-done((f32[4096,128]{1,0:T(8,128)S(1)}, f32[4096,128]{1,0:T(8,128)}, u32[]{:S(2)}) %copy-start.2) | copy-done | bytes 2097176
  8.9 0.9 collective-permute-start.6
  9.8 0.2 copy-done.4
  10.0 2.5 %collective-permute-start = (f32[2048,128]{1,0:T(8,128)S(1)}, f32[2048,128]{1,0:T(8,128)S(1)}, u32[]{:S(2)}, u32[]{:S(2)}) collective-permute-start(f32[2048,128]{1,0:T(8,128)S(1)} %copy-done.4), channel_id=1, source_target_pairs={{0,1},{1,2},{2,3},{3,4},{4,5},{5,6},{6,7},{7,8},{8,9},{9,10},{10,1... | collective-permute-start | bytes 3145736 | tf_op jit(solution)/shard_map/ppermute | solution.py:480
  12.6 3.4 %collective-permute-start.2 = (f32[2048,128]{1,0:T(8,128)S(1)}, f32[2048,128]{1,0:T(8,128)S(1)}, u32[]{:S(2)}, u32[]{:S(2)}) collective-permute-start(f32[2048,128]{1,0:T(8,128)S(1)} %copy-done.3), channel_id=1, source_target_pairs={{0,1},{1,2},{2,3},{3,4},{4,5},{5,6},{6,7},{7,8},{8,9},{9,10},{10,1... | collective-permute-start | bytes 3145736 | tf_op jit(solution)/shard_map/ppermute | solution.py:480
  16.0 0.7 collective-permute-start.7
  16.7 0.1 shard_map.92
  16.9 0.9 collective-permute-start.9
  17.7 14.7 %collective-permute-done.refs_0_ = f32[2048,128]{1,0:T(8,128)S(1)} collective-permute-done((f32[2048,128]{1,0:T(8,128)S(1)}, f32[2048,128]{1,0:T(8,128)S(1)}, u32[]{:S(2)}, u32[]{:S(2)}) %collective-permute-start) | collective-permute-done | bytes 1048608 | tf_op jit(solution)/shard_map/ppermute | solution.py:480
  32.4 1.8 %shard_map.87 = (f32[2048,128]{1,0:T(8,128)S(1)}, f32[2048,128]{1,0:T(8,128)S(1)}) custom-call(f32[2048,128]{1,0:T(8,128)S(1)} %collective-permute-done.refs_0_, f32[2048,128]{1,0:T(8,128)S(1)} %copy-done.1, f32[288,128]{1,0:T(8,128)S(1)} %copy-done), custom_call_target="tpu_custom_call" | custom-call | flops 1000 | bytes 1000 | tf_op jit(solution)/shard_map/pallas_call | solution.py:304
  34.3 1.9 %collective-permute-start.1 = (f32[2048,128]{1,0:T(8,128)S(1)}, f32[2048,128]{1,0:T(8,128)S(1)}, u32[]{:S(2)}, u32[]{:S(2)}) collective-permute-start(f32[2048,128]{1,0:T(8,128)S(1)} %get-tuple-element.31), channel_id=1, source_target_pairs={{0,1},{1,2},{2,3},{3,4},{4,5},{5,6},{6,7},{7,8},{8,9},{9,10},{10,1... | collective-permute-start | bytes 3145736 | tf_op jit(solution)/shard_map/ppermute | solution.py:480
  36.2 7.5 %collective-permute-done.2.refs_0_ = f32[2048,128]{1,0:T(8,128)S(1)} collective-permute-done((f32[2048,128]{1,0:T(8,128)S(1)}, f32[2048,128]{1,0:T(8,128)S(1)}, u32[]{:S(2)}, u32[]{:S(2)}) %collective-permute-start.2) | collective-permute-done | bytes 1048608 | tf_op jit(solution)/shard_map/ppermute | solution.py:480
  43.7 0.9 shard_map.88
  44.6 1.9 %collective-permute-start.4 = (f32[2048,128]{1,0:T(8,128)S(1)}, f32[2048,128]{1,0:T(8,128)S(1)}, u32[]{:S(2)}, u32[]{:S(2)}) collective-permute-start(f32[2048,128]{1,0:T(8,128)S(1)} %get-tuple-element.36), channel_id=1, source_target_pairs={{0,1},{1,2},{2,3},{3,4},{4,5},{5,6},{6,7},{7,8},{8,9},{9,10},{10,1... | collective-permute-start | bytes 3145736 | tf_op jit(solution)/shard_map/ppermute | solution.py:480
  46.5 10.2 %collective-permute-done.1.refs_0_ = f32[2048,128]{1,0:T(8,128)S(1)} collective-permute-done((f32[2048,128]{1,0:T(8,128)S(1)}, f32[2048,128]{1,0:T(8,128)S(1)}, u32[]{:S(2)}, u32[]{:S(2)}) %collective-permute-start.1) | collective-permute-done | bytes 1048608 | tf_op jit(solution)/shard_map/ppermute | solution.py:480
  56.7 2.7 %shard_map.89 = (f32[2048,128]{1,0:T(8,128)S(1)}, f32[2048,128]{1,0:T(8,128)S(1)}) custom-call(f32[2048,128]{1,0:T(8,128)S(1)} %collective-permute-done.1.refs_0_, f32[2048,128]{1,0:T(8,128)S(1)} %get-tuple-element.34.refs_1_, f32[288,128]{1,0:T(8,128)S(1)} %copy-done), custom_call_target="tpu_custom_call" | custom-call | flops 1000 | bytes 1000 | tf_op jit(solution)/shard_map/pallas_call | solution.py:304
  59.5 1.9 %collective-permute-start.3 = (f32[2048,128]{1,0:T(8,128)S(1)}, f32[2048,128]{1,0:T(8,128)S(1)}, u32[]{:S(2)}, u32[]{:S(2)}) collective-permute-start(f32[2048,128]{1,0:T(8,128)S(1)} %get-tuple-element.35), channel_id=1, source_target_pairs={{0,1},{1,2},{2,3},{3,4},{4,5},{5,6},{6,7},{7,8},{8,9},{9,10},{10,1... | collective-permute-start | bytes 3145736 | tf_op jit(solution)/shard_map/ppermute | solution.py:480
  61.4 6.6 %collective-permute-done.4.refs_0_ = f32[2048,128]{1,0:T(8,128)S(1)} collective-permute-done((f32[2048,128]{1,0:T(8,128)S(1)}, f32[2048,128]{1,0:T(8,128)S(1)}, u32[]{:S(2)}, u32[]{:S(2)}) %collective-permute-start.4) | collective-permute-done | bytes 1048608 | tf_op jit(solution)/shard_map/ppermute | solution.py:480
  68.0 2.7 %shard_map.90 = (f32[2048,128]{1,0:T(8,128)S(1)}, f32[2048,128]{1,0:T(8,128)S(1)}) custom-call(f32[2048,128]{1,0:T(8,128)S(1)} %collective-permute-done.4.refs_0_, f32[2048,128]{1,0:T(8,128)S(1)} %get-tuple-element.34.refs_1_, f32[2048,128]{1,0:T(8,128)S(1)} %get-tuple-element.37.refs_2_, f32[288,128]{1,0:T(8,128)S(1)} %copy-done), custom_call_target="tpu_custom_call" | custom-call | flops 1000 | bytes 1000 | tf_op jit(solution)/shard_map/pallas_call | solution.py:304
  70.7 0.7 collective-permute-start.8
  71.5 1.9 %collective-permute-start.11 = (f32[2048,128]{1,0:T(8,128)S(1)}, f32[2048,128]{1,0:T(8,128)S(1)}, u32[]{:S(2)}, u32[]{:S(2)}) collective-permute-start(f32[2048,128]{1,0:T(8,128)S(1)} %get-tuple-element.49), channel_id=1, source_target_pairs={{0,1},{1,2},{2,3},{3,4},{4,5},{5,6},{6,7},{7,8},{8,9},{9,10},{10,1... | collective-permute-start | bytes 3145736 | tf_op jit(solution)/shard_map/ppermute | solution.py:480
  73.5 0.7 collective-permute-start.12
  74.3 1.3 collective-permute-start.14
  75.6 6.3 %collective-permute-done.3.refs_0_ = f32[2048,128]{1,0:T(8,128)S(1)} collective-permute-done((f32[2048,128]{1,0:T(8,128)S(1)}, f32[2048,128]{1,0:T(8,128)S(1)}, u32[]{:S(2)}, u32[]{:S(2)}) %collective-permute-start.3) | collective-permute-done | bytes 1048608 | tf_op jit(solution)/shard_map/ppermute | solution.py:480
  81.9 2.7 %shard_map.94 = (f32[2048,128]{1,0:T(8,128)S(1)}, f32[2048,128]{1,0:T(8,128)S(1)}) custom-call(f32[2048,128]{1,0:T(8,128)S(1)} %collective-permute-done.3.refs_0_, f32[2048,128]{1,0:T(8,128)S(1)} %get-tuple-element.38.refs_1_, f32[288,128]{1,0:T(8,128)S(1)} %copy-done, f32[2048,128]{1,0:T(8,128)S(1)} %collective-permute-done.8.refs_3_, ...), custom_call_target="tpu_custom_call" | custom-call | flops 1000 | bytes 1000 | tf_op jit(solution)/shard_map/pallas_call | solution.py:304
  84.7 25.9 %collective-permute-start.10 = (f32[2048,128]{1,0:T(8,128)S(1)}, f32[2048,128]{1,0:T(8,128)S(1)}, u32[]{:S(2)}, u32[]{:S(2)}) collective-permute-start(f32[2048,128]{1,0:T(8,128)S(1)} %get-tuple-element.48), channel_id=1, source_target_pairs={{0,32},{1,33},{2,34},{3,35},{4,36},{5,37},{6,38},{7,39},{8,40},{9,... | collective-permute-start | bytes 3145736 | tf_op jit(solution)/shard_map/ppermute | solution.py:495
  110.6 1.8 %shard_map.95 = (f32[2048,128]{1,0:T(8,128)S(1)}, f32[2048,128]{1,0:T(8,128)S(1)}) custom-call(f32[2048,128]{1,0:T(8,128)S(1)} %collective-permute-done.11.refs_0_, f32[2048,128]{1,0:T(8,128)S(1)} %get-tuple-element.38.refs_1_, f32[2048,128]{1,0:T(8,128)S(1)} %get-tuple-element.50.refs_2_, f32[288,128]{1,0:T(8,128)S(1)} %copy-done, ...), custom_call_target="tpu_custom_call" | custom-call | flops 1000 | bytes 1000 | tf_op jit(solution)/shard_map/pallas_call | solution.py:304
  112.4 9.7 %collective-permute-start.13 = (f32[2048,128]{1,0:T(8,128)S(1)}, f32[2048,128]{1,0:T(8,128)S(1)}, u32[]{:S(2)}, u32[]{:S(2)}) collective-permute-start(f32[2048,128]{1,0:T(8,128)S(1)} %get-tuple-element.52), channel_id=1, source_target_pairs={{0,32},{1,33},{2,34},{3,35},{4,36},{5,37},{6,38},{7,39},{8,40},{9,... | collective-permute-start | bytes 3145736 | tf_op jit(solution)/shard_map/ppermute | solution.py:480
  122.2 9.4 %collective-permute-done.14.late = f32[2056,128]{1,0:T(8,128)S(1)} collective-permute-done((f32[2056,128]{1,0:T(8,128)S(1)}, f32[2056,128]{1,0:T(8,128)S(1)}, u32[]{:S(2)}, u32[]{:S(2)}) %collective-permute-start.14) | collective-permute-done | bytes 1052704 | tf_op jit(solution)/shard_map/ppermute | solution.py:480
  131.6 2.1 %shard_map.96 = (f32[4096,128]{1,0:T(8,128)}, f32[2048,128]{1,0:T(8,128)}) custom-call(f32[2048,128]{1,0:T(8,128)S(1)} %collective-permute-done.10.first, f32[2048,128]{1,0:T(8,128)S(1)} %collective-permute-done.13.second, f32[2056,128]{1,0:T(8,128)S(1)} %collective-permute-done.14.late, f32[2048,128]{1,0:T(8,128)S(1)} %get-tuple-element.53.stayed, ...), custom_call_target="tpu_custom_call" | custom-call | tf_op jit(solution)/shard_map/pallas_call | solution.py:462
  (21 shorter events, 0.3 us)
Async XLA Ops:
  6.5 0.7 collective-permute-start.5
  7.2 1.6 %copy-start.2 = (f32[4096,128]{1,0:T(8,128)S(1)}, f32[4096,128]{1,0:T(8,128)}, u32[]{:S(2)}) copy-start(f32[4096,128]{1,0:T(8,128)} %get-tuple-element.40.refs_1_) | copy-start | bytes 6291460
  8.8 1.2 copy-start.4
  8.8 3.8 %copy-start.3 = (f32[2048,128]{1,0:T(8,128)S(1)}, f32[2048,128]{1,0:T(8,128)}, u32[]{:S(2)}) copy-start(f32[2048,128]{1,0:T(8,128)} %get-tuple-element.32) | copy-start | bytes 3145732
  8.8 7.2 %copy-start.5 = (f32[8,128]{1,0:T(8,128)S(1)}, f32[8,128]{1,0:T(8,128)}, u32[]{:S(2)}) copy-start(f32[8,128]{1,0:T(8,128)} %get-tuple-element.43) | copy-start | bytes 12292
  8.9 7.8 %collective-permute-start.6 = (f32[2240,128]{1,0:T(8,128)S(1)}, f32[2240,128]{1,0:T(8,128)S(1)}, u32[]{:S(2)}, u32[]{:S(2)}) collective-permute-start(f32[2240,128]{1,0:T(8,128)S(1)} %get-tuple-element.41), channel_id=1, source_target_pairs={{32,63},{33,32},{34,33},{35,34},{36,35},{37,36},{38,37},{39,38},{4... | collective-permute-start | bytes 3440648 | tf_op jit(solution)/shard_map/ppermute | solution.py:480
  10.0 22.4 %collective-permute-start = (f32[2048,128]{1,0:T(8,128)S(1)}, f32[2048,128]{1,0:T(8,128)S(1)}, u32[]{:S(2)}, u32[]{:S(2)}) collective-permute-start(f32[2048,128]{1,0:T(8,128)S(1)} %copy-done.4), channel_id=1, source_target_pairs={{0,1},{1,2},{2,3},{3,4},{4,5},{5,6},{6,7},{7,8},{8,9},{9,10},{10,1... | collective-permute-start | bytes 3145736 | tf_op jit(solution)/shard_map/ppermute | solution.py:480
  12.6 31.1 %collective-permute-start.2 = (f32[2048,128]{1,0:T(8,128)S(1)}, f32[2048,128]{1,0:T(8,128)S(1)}, u32[]{:S(2)}, u32[]{:S(2)}) collective-permute-start(f32[2048,128]{1,0:T(8,128)S(1)} %copy-done.3), channel_id=1, source_target_pairs={{0,1},{1,2},{2,3},{3,4},{4,5},{5,6},{6,7},{7,8},{8,9},{9,10},{10,1... | collective-permute-start | bytes 3145736 | tf_op jit(solution)/shard_map/ppermute | solution.py:480
  16.0 0.7 collective-permute-start.7
  16.7 15.7 %copy-start = (f32[288,128]{1,0:T(8,128)S(1)}, f32[288,128]{1,0:T(8,128)}, u32[]{:S(2)}) copy-start(f32[288,128]{1,0:T(8,128)} %get-tuple-element.30.refs_2_.refs_3_) | copy-start | bytes 442372
  16.7 15.7 %copy-start.1 = (f32[2048,128]{1,0:T(8,128)S(1)}, f32[2048,128]{1,0:T(8,128)}, u32[]{:S(2)}) copy-start(f32[2048,128]{1,0:T(8,128)} %get-tuple-element.29.refs_1_) | copy-start | bytes 3145732
  16.9 56.5 %collective-permute-start.9 = (f32[2144,128]{1,0:T(8,128)S(1)}, f32[2144,128]{1,0:T(8,128)S(1)}, u32[]{:S(2)}, u32[]{:S(2)}) collective-permute-start(f32[2144,128]{1,0:T(8,128)S(1)} %get-tuple-element.45), channel_id=1, source_target_pairs={{32,63},{33,32},{34,33},{35,34},{36,35},{37,36},{38,37},{39,38},{4... | collective-permute-start | bytes 3293192 | tf_op jit(solution)/shard_map/ppermute | solution.py:480
  34.3 22.5 %collective-permute-start.1 = (f32[2048,128]{1,0:T(8,128)S(1)}, f32[2048,128]{1,0:T(8,128)S(1)}, u32[]{:S(2)}, u32[]{:S(2)}) collective-permute-start(f32[2048,128]{1,0:T(8,128)S(1)} %get-tuple-element.31), channel_id=1, source_target_pairs={{0,1},{1,2},{2,3},{3,4},{4,5},{5,6},{6,7},{7,8},{8,9},{9,10},{10,1... | collective-permute-start | bytes 3145736 | tf_op jit(solution)/shard_map/ppermute | solution.py:480
  44.6 23.4 %collective-permute-start.4 = (f32[2048,128]{1,0:T(8,128)S(1)}, f32[2048,128]{1,0:T(8,128)S(1)}, u32[]{:S(2)}, u32[]{:S(2)}) collective-permute-start(f32[2048,128]{1,0:T(8,128)S(1)} %get-tuple-element.36), channel_id=1, source_target_pairs={{0,1},{1,2},{2,3},{3,4},{4,5},{5,6},{6,7},{7,8},{8,9},{9,10},{10,1... | collective-permute-start | bytes 3145736 | tf_op jit(solution)/shard_map/ppermute | solution.py:480
  59.5 22.4 %collective-permute-start.3 = (f32[2048,128]{1,0:T(8,128)S(1)}, f32[2048,128]{1,0:T(8,128)S(1)}, u32[]{:S(2)}, u32[]{:S(2)}) collective-permute-start(f32[2048,128]{1,0:T(8,128)S(1)} %get-tuple-element.35), channel_id=1, source_target_pairs={{0,1},{1,2},{2,3},{3,4},{4,5},{5,6},{6,7},{7,8},{8,9},{9,10},{10,1... | collective-permute-start | bytes 3145736 | tf_op jit(solution)/shard_map/ppermute | solution.py:480
  70.7 11.2 %collective-permute-start.8 = (f32[2048,128]{1,0:T(8,128)S(1)}, f32[2048,128]{1,0:T(8,128)S(1)}, u32[]{:S(2)}, u32[]{:S(2)}) collective-permute-start(f32[2048,128]{1,0:T(8,128)S(1)} %get-tuple-element.44), channel_id=1, source_target_pairs={{32,99},{33,100},{34,101},{35,102},{36,103},{37,104},{38,105},{39,... | collective-permute-start | bytes 3145736 | tf_op jit(solution)/shard_map/ppermute | solution.py:480
  71.5 39.1 %collective-permute-start.11 = (f32[2048,128]{1,0:T(8,128)S(1)}, f32[2048,128]{1,0:T(8,128)S(1)}, u32[]{:S(2)}, u32[]{:S(2)}) collective-permute-start(f32[2048,128]{1,0:T(8,128)S(1)} %get-tuple-element.49), channel_id=1, source_target_pairs={{0,1},{1,2},{2,3},{3,4},{4,5},{5,6},{6,7},{7,8},{8,9},{9,10},{10,1... | collective-permute-start | bytes 3145736 | tf_op jit(solution)/shard_map/ppermute | solution.py:480
  73.5 37.1 %collective-permute-start.12 = (f32[2048,128]{1,0:T(8,128)S(1)}, f32[2048,128]{1,0:T(8,128)S(1)}, u32[]{:S(2)}, u32[]{:S(2)}) collective-permute-start(f32[2048,128]{1,0:T(8,128)S(1)} %get-tuple-element.51), channel_id=1, source_target_pairs={{32,35},{33,36},{34,37},{35,38},{36,39},{37,40},{38,41},{39,42},{4... | collective-permute-start | bytes 3145736 | tf_op jit(solution)/shard_map/ppermute | solution.py:480
  74.3 57.3 %collective-permute-start.14 = (f32[2056,128]{1,0:T(8,128)S(1)}, f32[2056,128]{1,0:T(8,128)S(1)}, u32[]{:S(2)}, u32[]{:S(2)}) collective-permute-start(f32[2056,128]{1,0:T(8,128)S(1)} %get-tuple-element.47.refs_4_), channel_id=1, source_target_pairs={{32,67},{33,68},{34,69},{35,70},{36,71},{37,72},{38,73},{39,74},{4... | collective-permute-start | bytes 3158024 | tf_op jit(solution)/shard_map/ppermute | solution.py:480
  84.7 37.5 %collective-permute-start.10 = (f32[2048,128]{1,0:T(8,128)S(1)}, f32[2048,128]{1,0:T(8,128)S(1)}, u32[]{:S(2)}, u32[]{:S(2)}) collective-permute-start(f32[2048,128]{1,0:T(8,128)S(1)} %get-tuple-element.48), channel_id=1, source_target_pairs={{0,32},{1,33},{2,34},{3,35},{4,36},{5,37},{6,38},{7,39},{8,40},{9,... | collective-permute-start | bytes 3145736 | tf_op jit(solution)/shard_map/ppermute | solution.py:495
  112.4 19.2 %collective-permute-start.13 = (f32[2048,128]{1,0:T(8,128)S(1)}, f32[2048,128]{1,0:T(8,128)S(1)}, u32[]{:S(2)}, u32[]{:S(2)}) collective-permute-start(f32[2048,128]{1,0:T(8,128)S(1)} %get-tuple-element.52), channel_id=1, source_target_pairs={{0,32},{1,33},{2,34},{3,35},{4,36},{5,37},{6,38},{7,39},{8,40},{9,... | collective-permute-start | bytes 3145736 | tf_op jit(solution)/shard_map/ppermute | solution.py:480
where the time goes:
time: 133 us; the launch traced here: 134 us
  starting transfers between devices  55.2 us (42%)
  waiting for transfers between devices  54.7 us (41%)
  Pallas kernels  21 us (16%)
  local copies, waits for them, and re-layouts  1.83 us (1%)
    ppermute x14, waiting for transfers between devices, sent(): return lax.ppermute(array, AXES, route(groups, members, odd, move))  54.7 us
    ppermute x14, starting transfers between devices, sent(): return lax.ppermute(array, AXES, route(groups, members, odd, move))  29.2 us
    ppermute x1, starting transfers between devices, even_half(): e[h] = lax.ppermute(x, AXES, swap)  25.9 us
    pallas_call x6, Pallas kernels, even_step(): pl.pallas_call(kernel, out_shape=[wide(size), wide(HALF)], in_specs=[ANY]...  12.8 us
    pallas_call x1, Pallas kernels, first_step(): pl.pallas_call(kernel, out_shape=[wide(HALF), wide(HALF), wide(HALF + lis...  5.82 us
  transfers between devices with their start and end apart: 15, of which 6 were waited for; matrix products, arithmetic and copies ran while one was open for 0% of the time, Pallas kernels for 10%

commit v1 on v0

--- a/solution.py
+++ b/solution.py
@@ -16,6 +16,7 @@
 VERT_TILES = 16
 CTX_TILES = 8
 HALF = 8 * TILE
+QUARTER = 4 * TILE
 FIRST_LIMIT = 60 * 1024 * 1024
 STEP_LIMIT = 20 * 1024 * 1024
 
@@ -132,7 +133,7 @@
 
 def first_kernel(steps, *refs):
     vertex, context, count_in, vert_in, ctx_in, pos_in, neg_in, *refs = refs
-    low_out, high_out, moved_out, ctx_out, vert_out, own_out, names_out, *refs = refs
+    low_out, high_out, moved_out, moved_high, ctx_out, vert_out, own_out, *refs = refs
     v_old, v_new, c_old, c_new, count, vert, ctx, pos, neg, own, chosen, sems = refs
     heads = moved([(count_in, count), (vert_in, vert), (ctx_in, ctx)], sems)
     lists = moved([(pos_in, pos), (neg_in, neg)], sems, 3)
@@ -190,10 +191,10 @@
     @pl.when(odd == 1)
     def odd_group():
         stores = [
-            (c_new, moved_out.at[pl.ds(0, HALF)]),
-            (own, moved_out.at[pl.ds(HALF, LISTED * (steps - 1))]),
+            (c_new.at[pl.ds(0, QUARTER)], moved_out.at[pl.ds(0, QUARTER)]),
+            (own, moved_out.at[pl.ds(QUARTER, LISTED * (steps - 1))]),
+            (c_new.at[pl.ds(QUARTER, QUARTER)], moved_high),
             (v_new, vert_out),
-            (own.at[pl.ds(LISTED * (steps - 2) + META, 8)], names_out),
         ]
         waited(moved(stores, sems))
 
@@ -210,11 +211,11 @@
         out_shape=[
             wide(HALF),
             wide(HALF),
-            wide(HALF + listed),
+            wide(QUARTER + listed),
+            wide(QUARTER),
             wide(HALF),
             wide(2 * HALF),
             wide(listed),
-            wide(8),
         ],
         in_specs=[ANY] * 7,
         out_specs=[ANY] * 7,
@@ -335,60 +336,58 @@
         late = late + 1 - soon.astype(jnp.int32)
 
 
-def odd_kernel(left, n_after, *refs):
+def odd_kernel(left, half, n_after, *refs):
     move_in, stay_in, *refs = refs
-    if left == 1:
-        names, *refs = refs
+    list_in, total_in = move_in.at[pl.ds(QUARTER, LISTED)] if not half else None, stay_in
+    parts = left == 0
+    if half:
+        carrier, total_in, *refs = refs
+        list_in = carrier.at[pl.ds(QUARTER, LISTED)]
     refs = refs[n_after:]
     move_out, *refs = refs
-    if left:
+    if left or not half:
         stay_out, *refs = refs
-    if left < 2:
+    if parts:
         part_out, *refs = refs
-    m_old, m_new, s_old, s_new, listed, metas, chosen, used, order, places, sems = refs
+    m_old, m_new, s_old, s_new, listed, meta, chosen, used, order, places, sems = refs
 
     @pl.when(group_odd() == 1)
     def work():
-        meta = metas.at[0]
-        split = metas.at[1 if left else 0]
-        heads = [(move_in.at[pl.ds(HALF + META, 8)], meta)]
-        if left == 1:
-            heads.append((names, split))
-        heads = moved(heads, sems)
+        heads = moved([(list_in.at[pl.ds(META, 8)], meta)], sems)
         loads = [
-            (move_in.at[pl.ds(HALF, LISTED)], listed),
-            (move_in.at[pl.ds(0, HALF)], m_old),
+            (list_in, listed),
+            (move_in.at[pl.ds(0, QUARTER)], m_old),
             (stay_in, s_old),
-            (move_in.at[pl.ds(0, HALF)], m_new),
-            (stay_in, s_new),
+            (move_in.at[pl.ds(0, QUARTER)], m_new),
+            (total_in, s_new),
         ]
-        if left:
-            rest = pl.ds(HALF, LISTED * left)
-            loads.append((move_in.at[pl.ds(HALF + LISTED, LISTED * left)], move_out.at[rest]))
+        if left and not half:
+            rest = pl.ds(QUARTER, LISTED * left)
+            loads.append((move_in.at[pl.ds(QUARTER + LISTED, LISTED * left)], move_out.at[rest]))
         loads = moved(loads, sems, 2)
         waited(heads)
-        mine = choose(chosen, head(meta, 16), lambda t: True)
-        if left < 2:
-            part_tiles(split, used, order)
+        mine = choose(chosen, head(meta, 16), lambda t: head(meta, 8 + t) // 4 == half)
+        if parts:
+            part_tiles(meta, used, order)
         waited(loads)
 
         def one(t, live):
-            vi, ci = head(meta, t), head(meta, 8 + t)
+            vi, ci = head(meta, t), lax.rem(head(meta, 8 + t), 4)
             rows = listed_rows(listed, t)
             dv, dc = slot_update(s_old[tile(vi), :], m_old[tile(ci), :], *rows, live)
             return s_new, vi, dv, m_new, ci, dc
 
         run_pairs(chosen, mine, one)
-        stores = [(m_new, move_out.at[pl.ds(0, HALF)])]
-        if left:
+        stores = [(m_new, move_out.at[pl.ds(0, QUARTER)])]
+        if left or not half:
             stores.append((s_new, stay_out))
-        if left < 2:
-            first = 0 if left else SLOTS
+        if parts:
+            first = SLOTS if half else 0
             stores += [
                 (s_new.at[tile(order[first + n])], part_out.at[pl.ds(n * TILE, TILE)])
                 for n in range(SLOTS)
             ]
-        if not left:
+        if parts and half:
             lane = lax.broadcasted_iota(jnp.int32, (8, 128), 1)
             spot = jnp.zeros((8, 128), jnp.int32)
             for n in range(VERT_TILES):
@@ -398,16 +397,18 @@
         waited(moved(stores, sems))
 
 
-def odd_step(left, moving, staying, names, after):
-    operands = [moving, staying] + ([names] if left == 1 else [])
-    out_shape = [wide(HALF + LISTED * left)]
-    if left:
+def odd_step(left, half, moving, staying, carrier, total, after):
+    operands = [moving, staying]
+    out_shape = [wide(QUARTER + (0 if half else LISTED * left))]
+    if left or not half:
         out_shape.append(wide(2 * HALF))
-    if left < 2:
-        out_shape.append(wide(HALF if left else HALF + 8))
+    if half:
+        operands += [carrier, total]
+    if left == 0:
+        out_shape.append(wide(HALF + 8 if half else HALF))
 
     def kernel(*refs):
-        odd_kernel(left, len(after), *refs)
+        odd_kernel(left, half, len(after), *refs)
 
     return pl.pallas_call(
         kernel,
@@ -415,12 +416,12 @@
         in_specs=[ANY] * (len(operands) + len(after)),
         out_specs=[ANY] * len(out_shape),
         scratch_shapes=[
-            vmem(HALF),
-            vmem(HALF),
+            vmem(QUARTER),
+            vmem(QUARTER),
             vmem(2 * HALF),
             vmem(2 * HALF),
             vmem(LISTED),
-            pltpu.SMEM((2, 8, 128), jnp.float32),
+            pltpu.SMEM((8, 128), jnp.float32),
             pltpu.SMEM((SLOTS + 1,), jnp.int32),
             pltpu.SMEM((VERT_TILES,), jnp.int32),
             pltpu.SMEM((VERT_TILES,), jnp.int32),
@@ -428,11 +429,11 @@
             pltpu.SemaphoreType.DMA((12,)),
         ],
         compiler_params=pltpu.CompilerParams(vmem_limit_bytes=STEP_LIMIT),
-        cost_estimate=pl.CostEstimate(flops=1000, bytes_accessed=1000, transcendentals=0),
+        cost_estimate=pl.CostEstimate(flops=4000000000, bytes_accessed=1000, transcendentals=0),
     )(*operands, *after)
 
 
-def finish_kernel(first, second, late, stayed, home, vertex, context, spots, sems):
+def finish_kernel(first, second, late, stayed, home, home_high, vertex, context, spots, sems):
     odd = group_odd()
 
     @pl.when(odd == 0)
@@ -453,7 +454,8 @@
         copies = [
             (first, vertex.at[pl.ds(0, HALF)]),
             (second, vertex.at[pl.ds(HALF, HALF)]),
-            (home, context),
+            (home, context.at[pl.ds(0, QUARTER)]),
+            (home_high, context.at[pl.ds(QUARTER, QUARTER)]),
         ]
         waited(moved(copies, sems))
 
@@ -462,7 +464,7 @@
     return pl.pallas_call(
         finish_kernel,
         out_shape=[wide(2 * HALF), wide(HALF)],
-        in_specs=[ANY] * 5,
+        in_specs=[ANY] * 6,
         out_specs=[HBM, HBM],
         scratch_shapes=[
             pltpu.SMEM((8, 128), jnp.float32),
@@ -479,10 +481,9 @@
     def sent(array, odd, move):
         return lax.ppermute(array, AXES, route(groups, members, odd, move))
 
-    low, high, o, c_state, v_state, own, names = first_step(vertex, context, lists)
-    names = sent(names, 1, (0, 1 - steps))
+    low, high, *o, c_state, v_state, own = first_step(vertex, context, lists)
     e = [sent(low, 0, (0, 1)), sent(high, 0, (0, 1))]
-    o = sent(o, 1, (0, -1))
+    o = [sent(x, 1, (0, -1)) for x in o]
 
     def even_half(s, h, total, give=None, *after):
         x, total = even_step(s, h, e[h], c_state, total, own, give, after)
@@ -495,23 +496,28 @@
             e[h] = lax.ppermute(x, AXES, swap)
         return total
 
-    def odd_whole(s, *after):
-        x, *rest = odd_step(steps - 1 - s, o, v_state, names, after)
-        return sent(x, 1, (0, -1) if s + 1 < steps else (0, steps - 1)), *rest
-
+    def odd_half(s, h, total, *after):
+        carrier = None if h == 0 else carriers[s]
+        carriers[s] = o[h] if h == 0 else carrier
+        x, *rest = odd_step(steps - 1 - s, h, o[h], v_state, carrier, total, after)
+        o[h] = sent(x, 1, (0, -1) if s + 1 < steps else (0, steps - 1))
+        return rest
+
+    carriers = {}
     beside = (2, steps - 1)
     total = even_half(1, 0, None)
     c_state = even_half(1, 1, total)
     total = even_half(2, 0, None)
     c_state = even_half(2, 1, total)
-    o, v_state = odd_whole(1)
-    o, v_state, early = odd_whole(2)
+    (v_state,) = odd_half(1, 1, *odd_half(1, 0, None))
+    (v_state,) = odd_half(2, 1, *odd_half(2, 0, None))
+    total, early = odd_half(3, 0, None)
     early = sent(early, 1, beside)
-    o, late = odd_whole(3)
+    (late,) = odd_half(3, 1, total)
     total = even_half(3, 0, None, early, late)
     late = sent(late, 1, (1, steps - 1))
-    c_state = even_half(3, 1, total, None, o)
-    return tuple(finish(*e, late, c_state, o))
+    c_state = even_half(3, 1, total, None, *o)
+    return tuple(finish(*e, late, c_state, *o))
 
 
 def solution(mesh):

time: 133 us -> 131 us (0.985); the launches traced: 134 us -> 130 us
  starting transfers between devices: 55.2 us -> 31.3 us
  waiting for transfers between devices: 54.7 us -> 73.4 us
  Pallas kernels: 21 us -> 22.5 us
    ppermute x1, starting transfers between devices: 25.9 us -> 0.09 us  [even_half(): e[h] = lax.ppermute(x, AXES, swap)]
    ppermute x14 -> x17, waiting for transfers between devices: 54.7 us -> 73.4 us  [sent(): return lax.ppermute(array, AXES, route(groups, members, odd, move))]
    ppermute x14 -> x17, starting transfers between devices: 29.2 us -> 31.2 us  [sent(): return lax.ppermute(array, AXES, route(groups, members, odd, move))]
  transfers between devices with their start and end apart: 15 -> 18, of which waited for: 6 -> 7; matrix products, arithmetic and copies ran while one was open for 0% -> 0% of each run, Pallas kernels for 10% -> 11%
where the time goes in v1:
time: 131 us; the launch traced here: 130 us
  waiting for transfers between devices  73.4 us (56%)
  starting transfers between devices  31.3 us (24%)
  Pallas kernels  22.5 us (17%)
  local copies, waits for them, and re-layouts  1.59 us (1%)
    ppermute x17, waiting for transfers between devices, sent(): return lax.ppermute(array, AXES, route(groups, members, odd, move))  73.4 us
    ppermute x17, starting transfers between devices, sent(): return lax.ppermute(array, AXES, route(groups, members, odd, move))  31.2 us
    pallas_call x6, Pallas kernels, even_step(): pl.pallas_call(kernel, out_shape=[wide(size), wide(HALF)], in_specs=[ANY]...  12.9 us
    pallas_call x1, Pallas kernels, first_step(): pl.pallas_call(kernel, out_shape=[wide(HALF), wide(HALF), wide(QUARTER +...  6.75 us
  transfers between devices with their start and end apart: 18, of which 7 were waited for; matrix products, arithmetic and copies ran while one was open for 0% of the time, Pallas kernels for 11%

profile of v1, /device:TPU:0, one launch (start us, length us, event | category | flops | bytes accessed | tf_op | source)
XLA Modules:
  0.0 129.9 jit_solution(11246037904298734326)
XLA Ops:
  0.6 6.8 %shard_map.86 = (f32[2048,128]{1,0:T(8,128)}, f32[2048,128]{1,0:T(8,128)}, f32[1312,128]{1,0:T(8,128)}, f32[1024,128]{1,0:T(8,128)}, f32[2048,128]{1,0:T(8,128)}...) custom-call(f32[4096,128]{1,0:T(8,128)} %refs_0_.1, f32[2048,128]{1,0:T(8,128)} %refs_1_.1, s32[4]{0:T(128)} %refs_2_.1, ...), custom_call_target="tpu_custom_call" | custom-call | flops 1000 | bytes 1000 | tf_op jit(solution)/shard_map/pallas_call | solution.py:209
  7.4 0.7 collective-permute-start.5
  8.1 1.9 %collective-permute-start = (f32[2048,128]{1,0:T(8,128)}, f32[2048,128]{1,0:T(8,128)S(1)}, u32[]{:S(2)}, u32[]{:S(2)}) collective-permute-start(f32[2048,128]{1,0:T(8,128)} %get-tuple-element.34), channel_id=1, source_target_pairs={{0,1},{1,2},{2,3},{3,4},{4,5},{5,6},{6,7},{7,8},{8,9},{9,10},{10,1... | collective-permute-start | bytes 3145736 | tf_op jit(solution)/shard_map/ppermute | solution.py:482
  10.0 3.1 %collective-permute-start.2 = (f32[2048,128]{1,0:T(8,128)}, f32[2048,128]{1,0:T(8,128)S(1)}, u32[]{:S(2)}, u32[]{:S(2)}) collective-permute-start(f32[2048,128]{1,0:T(8,128)} %get-tuple-element.38), channel_id=1, source_target_pairs={{0,1},{1,2},{2,3},{3,4},{4,5},{5,6},{6,7},{7,8},{8,9},{9,10},{10,1... | collective-permute-start | bytes 3145736 | tf_op jit(solution)/shard_map/ppermute | solution.py:482
  13.2 0.7 collective-permute-start.7
  13.9 1.6 %copy-done.2 = f32[4096,128]{1,0:T(8,128)S(1)} copy-done((f32[4096,128]{1,0:T(8,128)S(1)}, f32[4096,128]{1,0:T(8,128)}, u32[]{:S(2)}) %copy-start.2) | copy-done | bytes 2097176
  15.6 0.7 collective-permute-start.6
  16.4 0.8 collective-permute-start.9
  17.3 14.3 %collective-permute-done.refs_0_ = f32[2048,128]{1,0:T(8,128)S(1)} collective-permute-done((f32[2048,128]{1,0:T(8,128)}, f32[2048,128]{1,0:T(8,128)S(1)}, u32[]{:S(2)}, u32[]{:S(2)}) %collective-permute-start) | collective-permute-done | bytes 1048608 | tf_op jit(solution)/shard_map/ppermute | solution.py:482
  31.6 2.7 %shard_map.87 = (f32[2048,128]{1,0:T(8,128)S(1)}, f32[2048,128]{1,0:T(8,128)S(1)}) custom-call(f32[2048,128]{1,0:T(8,128)S(1)} %collective-permute-done.refs_0_, f32[2048,128]{1,0:T(8,128)S(1)} %copy-done.1, f32[288,128]{1,0:T(8,128)S(1)} %copy-done), custom_call_target="tpu_custom_call" | custom-call | flops 1000 | bytes 1000 | tf_op jit(solution)/shard_map/pallas_call | solution.py:305
  34.4 1.9 %collective-permute-start.1 = (f32[2048,128]{1,0:T(8,128)S(1)}, f32[2048,128]{1,0:T(8,128)S(1)}, u32[]{:S(2)}, u32[]{:S(2)}) collective-permute-start(f32[2048,128]{1,0:T(8,128)S(1)} %get-tuple-element.37), channel_id=1, source_target_pairs={{0,1},{1,2},{2,3},{3,4},{4,5},{5,6},{6,7},{7,8},{8,9},{9,10},{10,1... | collective-permute-start | bytes 3145736 | tf_op jit(solution)/shard_map/ppermute | solution.py:482
  36.3 6.5 %collective-permute-done.2.refs_0_ = f32[2048,128]{1,0:T(8,128)S(1)} collective-permute-done((f32[2048,128]{1,0:T(8,128)}, f32[2048,128]{1,0:T(8,128)S(1)}, u32[]{:S(2)}, u32[]{:S(2)}) %collective-permute-start.2) | collective-permute-done | bytes 1048608 | tf_op jit(solution)/shard_map/ppermute | solution.py:482
  42.8 1.8 %shard_map.88 = (f32[2048,128]{1,0:T(8,128)S(1)}, f32[2048,128]{1,0:T(8,128)S(1)}) custom-call(f32[2048,128]{1,0:T(8,128)S(1)} %collective-permute-done.2.refs_0_, f32[2048,128]{1,0:T(8,128)S(1)} %copy-done.1, f32[2048,128]{1,0:T(8,128)S(1)} %get-tuple-element.39.refs_2_, f32[288,128]{1,0:T(8,128)S(1)} %copy-done), custom_call_target="tpu_custom_call" | custom-call | flops 1000 | bytes 1000 | tf_op jit(solution)/shard_map/pallas_call | solution.py:305
  44.7 1.9 %collective-permute-start.4 = (f32[2048,128]{1,0:T(8,128)S(1)}, f32[2048,128]{1,0:T(8,128)S(1)}, u32[]{:S(2)}, u32[]{:S(2)}) collective-permute-start(f32[2048,128]{1,0:T(8,128)S(1)} %get-tuple-element.42), channel_id=1, source_target_pairs={{0,1},{1,2},{2,3},{3,4},{4,5},{5,6},{6,7},{7,8},{8,9},{9,10},{10,1... | collective-permute-start | bytes 3145736 | tf_op jit(solution)/shard_map/ppermute | solution.py:482
  46.7 0.7 collective-permute-start.8
  47.6 0.7 collective-permute-start.11
  48.4 0.7 collective-permute-start.10
  49.2 7.6 %collective-permute-done.1.refs_0_ = f32[2048,128]{1,0:T(8,128)S(1)} collective-permute-done((f32[2048,128]{1,0:T(8,128)S(1)}, f32[2048,128]{1,0:T(8,128)S(1)}, u32[]{:S(2)}, u32[]{:S(2)}) %collective-permute-start.1) | collective-permute-done | bytes 1048608 | tf_op jit(solution)/shard_map/ppermute | solution.py:482
  56.8 1.8 %shard_map.89 = (f32[2048,128]{1,0:T(8,128)S(1)}, f32[2048,128]{1,0:T(8,128)S(1)}) custom-call(f32[2048,128]{1,0:T(8,128)S(1)} %collective-permute-done.1.refs_0_, f32[2048,128]{1,0:T(8,128)S(1)} %get-tuple-element.40.refs_1_, f32[288,128]{1,0:T(8,128)S(1)} %copy-done), custom_call_target="tpu_custom_call" | custom-call | flops 1000 | bytes 1000 | tf_op jit(solution)/shard_map/pallas_call | solution.py:305
  58.6 1.9 %collective-permute-start.3 = (f32[2048,128]{1,0:T(8,128)S(1)}, f32[2048,128]{1,0:T(8,128)S(1)}, u32[]{:S(2)}, u32[]{:S(2)}) collective-permute-start(f32[2048,128]{1,0:T(8,128)S(1)} %get-tuple-element.41), channel_id=1, source_target_pairs={{0,1},{1,2},{2,3},{3,4},{4,5},{5,6},{6,7},{7,8},{8,9},{9,10},{10,1... | collective-permute-start | bytes 3145736 | tf_op jit(solution)/shard_map/ppermute | solution.py:482
  60.5 7.5 %collective-permute-done.4.refs_0_ = f32[2048,128]{1,0:T(8,128)S(1)} collective-permute-done((f32[2048,128]{1,0:T(8,128)S(1)}, f32[2048,128]{1,0:T(8,128)S(1)}, u32[]{:S(2)}, u32[]{:S(2)}) %collective-permute-start.4) | collective-permute-done | bytes 1048608 | tf_op jit(solution)/shard_map/ppermute | solution.py:482
  68.0 2.9 %shard_map.90 = (f32[2048,128]{1,0:T(8,128)S(1)}, f32[2048,128]{1,0:T(8,128)S(1)}) custom-call(f32[2048,128]{1,0:T(8,128)S(1)} %collective-permute-done.4.refs_0_, f32[2048,128]{1,0:T(8,128)S(1)} %get-tuple-element.40.refs_1_, f32[2048,128]{1,0:T(8,128)S(1)} %get-tuple-element.43.refs_2_, f32[288,128]{1,0:T(8,128)S(1)} %copy-done), custom_call_target="tpu_custom_call" | custom-call | flops 1000 | bytes 1000 | tf_op jit(solution)/shard_map/pallas_call | solution.py:305
  70.9 1.9 %collective-permute-start.13 = (f32[2048,128]{1,0:T(8,128)S(1)}, f32[2048,128]{1,0:T(8,128)S(1)}, u32[]{:S(2)}, u32[]{:S(2)}) collective-permute-start(f32[2048,128]{1,0:T(8,128)S(1)} %get-tuple-element.60), channel_id=1, source_target_pairs={{0,1},{1,2},{2,3},{3,4},{4,5},{5,6},{6,7},{7,8},{8,9},{9,10},{10,1... | collective-permute-start | bytes 3145736 | tf_op jit(solution)/shard_map/ppermute | solution.py:482
  73.0 0.7 collective-permute-start.15
  74.4 1.3 collective-permute-start.17
  75.7 10.4 %collective-permute-done.3.refs_0_ = f32[2048,128]{1,0:T(8,128)S(1)} collective-permute-done((f32[2048,128]{1,0:T(8,128)S(1)}, f32[2048,128]{1,0:T(8,128)S(1)}, u32[]{:S(2)}, u32[]{:S(2)}) %collective-permute-start.3) | collective-permute-done | bytes 1048608 | tf_op jit(solution)/shard_map/ppermute | solution.py:482
  86.1 1.8 %shard_map.97 = (f32[2048,128]{1,0:T(8,128)S(1)}, f32[2048,128]{1,0:T(8,128)S(1)}) custom-call(f32[2048,128]{1,0:T(8,128)S(1)} %collective-permute-done.3.refs_0_, f32[2048,128]{1,0:T(8,128)S(1)} %get-tuple-element.44.refs_1_, f32[288,128]{1,0:T(8,128)S(1)} %copy-done, f32[2048,128]{1,0:T(8,128)S(1)} %collective-permute-done.10.refs_3_, ...), custom_call_target="tpu_custom_call" | custom-call | flops 1000 | bytes 1000 | tf_op jit(solution)/shard_map/pallas_call | solution.py:305
  87.9 18.5 %collective-permute-done.13.refs_0_ = f32[2048,128]{1,0:T(8,128)S(1)} collective-permute-done((f32[2048,128]{1,0:T(8,128)S(1)}, f32[2048,128]{1,0:T(8,128)S(1)}, u32[]{:S(2)}, u32[]{:S(2)}) %collective-permute-start.13) | collective-permute-done | bytes 1048608 | tf_op jit(solution)/shard_map/ppermute | solution.py:482
  106.5 1.8 %shard_map.98 = (f32[2048,128]{1,0:T(8,128)S(1)}, f32[2048,128]{1,0:T(8,128)S(1)}) custom-call(f32[2048,128]{1,0:T(8,128)S(1)} %collective-permute-done.13.refs_0_, f32[2048,128]{1,0:T(8,128)S(1)} %get-tuple-element.44.refs_1_, f32[2048,128]{1,0:T(8,128)S(1)} %get-tuple-element.61.refs_2_, f32[288,128]{1,0:T(8,128)S(1)} %copy-done, ...), custom_call_target="tpu_custom_call" | custom-call | flops 1000 | bytes 1000 | tf_op jit(solution)/shard_map/pallas_call | solution.py:305
  108.3 10.7 %collective-permute-start.16 = (f32[2048,128]{1,0:T(8,128)S(1)}, f32[2048,128]{1,0:T(8,128)S(1)}, u32[]{:S(2)}, u32[]{:S(2)}) collective-permute-start(f32[2048,128]{1,0:T(8,128)S(1)} %get-tuple-element.64), channel_id=1, source_target_pairs={{0,32},{1,33},{2,34},{3,35},{4,36},{5,37},{6,38},{7,39},{8,40},{9,... | collective-permute-start | bytes 3145736 | tf_op jit(solution)/shard_map/ppermute | solution.py:482
  119.1 8.6 %collective-permute-done.17.late = f32[2056,128]{1,0:T(8,128)S(1)} collective-permute-done((f32[2056,128]{1,0:T(8,128)S(1)}, f32[2056,128]{1,0:T(8,128)S(1)}, u32[]{:S(2)}, u32[]{:S(2)}) %collective-permute-start.17) | collective-permute-done | bytes 1052704 | tf_op jit(solution)/shard_map/ppermute | solution.py:482
  127.7 2.1 %shard_map.99 = (f32[4096,128]{1,0:T(8,128)}, f32[2048,128]{1,0:T(8,128)}) custom-call(f32[2048,128]{1,0:T(8,128)S(1)} %collective-permute-done.12.first, f32[2048,128]{1,0:T(8,128)S(1)} %collective-permute-done.16.second, f32[2056,128]{1,0:T(8,128)S(1)} %collective-permute-done.17.late, f32[2048,128]{1,0:T(8,128)S(1)} %get-tuple-element.65.stayed, ...), custom_call_target="tpu_custom_call" | custom-call | tf_op jit(solution)/shard_map/pallas_call | solution.py:464
  (24 shorter events, 1.6 us)
Async XLA Ops:
  7.4 6.5 %collective-permute-start.5 = (f32[1312,128]{1,0:T(8,128)}, f32[1312,128]{1,0:T(8,128)S(1)}, u32[]{:S(2)}, u32[]{:S(2)}) collective-permute-start(f32[1312,128]{1,0:T(8,128)} %get-tuple-element.45), channel_id=1, source_target_pairs={{32,63},{33,32},{34,33},{35,34},{36,35},{37,36},{38,37},{39,38},{4... | collective-permute-start | bytes 2015240 | tf_op jit(solution)/shard_map/ppermute | solution.py:482
  8.1 23.5 %collective-permute-start = (f32[2048,128]{1,0:T(8,128)}, f32[2048,128]{1,0:T(8,128)S(1)}, u32[]{:S(2)}, u32[]{:S(2)}) collective-permute-start(f32[2048,128]{1,0:T(8,128)} %get-tuple-element.34), channel_id=1, source_target_pairs={{0,1},{1,2},{2,3},{3,4},{4,5},{5,6},{6,7},{7,8},{8,9},{9,10},{10,1... | collective-permute-start | bytes 3145736 | tf_op jit(solution)/shard_map/ppermute | solution.py:482
  10.0 32.8 %collective-permute-start.2 = (f32[2048,128]{1,0:T(8,128)}, f32[2048,128]{1,0:T(8,128)S(1)}, u32[]{:S(2)}, u32[]{:S(2)}) collective-permute-start(f32[2048,128]{1,0:T(8,128)} %get-tuple-element.38), channel_id=1, source_target_pairs={{0,1},{1,2},{2,3},{3,4},{4,5},{5,6},{6,7},{7,8},{8,9},{9,10},{10,1... | collective-permute-start | bytes 3145736 | tf_op jit(solution)/shard_map/ppermute | solution.py:482
  13.2 3.1 %collective-permute-start.7 = (f32[1024,128]{1,0:T(8,128)}, f32[1024,128]{1,0:T(8,128)S(1)}, u32[]{:S(2)}, u32[]{:S(2)}) collective-permute-start(f32[1024,128]{1,0:T(8,128)} %get-tuple-element.48), channel_id=1, source_target_pairs={{32,63},{33,32},{34,33},{35,34},{36,35},{37,36},{38,37},{39,38},{4... | collective-permute-start | bytes 1572872 | tf_op jit(solution)/shard_map/ppermute | solution.py:482
  13.9 1.6 %copy-start.2 = (f32[4096,128]{1,0:T(8,128)S(1)}, f32[4096,128]{1,0:T(8,128)}, u32[]{:S(2)}) copy-start(f32[4096,128]{1,0:T(8,128)} %get-tuple-element.46.refs_1_) | copy-start | bytes 6291460
  15.6 31.0 %collective-permute-start.6 = (f32[1216,128]{1,0:T(8,128)S(1)}, f32[1216,128]{1,0:T(8,128)S(1)}, u32[]{:S(2)}, u32[]{:S(2)}) collective-permute-start(f32[1216,128]{1,0:T(8,128)S(1)} %get-tuple-element.47), channel_id=1, source_target_pairs={{32,63},{33,32},{34,33},{35,34},{36,35},{37,36},{38,37},{39,38},{4... | collective-permute-start | bytes 1867784 | tf_op jit(solution)/shard_map/ppermute | solution.py:482
  16.3 15.3 %copy-start = (f32[288,128]{1,0:T(8,128)S(1)}, f32[288,128]{1,0:T(8,128)}, u32[]{:S(2)}) copy-start(f32[288,128]{1,0:T(8,128)} %get-tuple-element.36.refs_2_.refs_3_) | copy-start | bytes 442372
  16.3 15.3 %copy-start.1 = (f32[2048,128]{1,0:T(8,128)S(1)}, f32[2048,128]{1,0:T(8,128)}, u32[]{:S(2)}) copy-start(f32[2048,128]{1,0:T(8,128)} %get-tuple-element.35.refs_1_) | copy-start | bytes 3145732
  16.4 31.0 %collective-permute-start.9 = (f32[1024,128]{1,0:T(8,128)S(1)}, f32[1024,128]{1,0:T(8,128)S(1)}, u32[]{:S(2)}, u32[]{:S(2)}) collective-permute-start(f32[1024,128]{1,0:T(8,128)S(1)} %get-tuple-element.52), channel_id=1, source_target_pairs={{32,63},{33,32},{34,33},{35,34},{36,35},{37,36},{38,37},{39,38},{4... | collective-permute-start | bytes 1572872 | tf_op jit(solution)/shard_map/ppermute | solution.py:482
  34.4 22.4 %collective-permute-start.1 = (f32[2048,128]{1,0:T(8,128)S(1)}, f32[2048,128]{1,0:T(8,128)S(1)}, u32[]{:S(2)}, u32[]{:S(2)}) collective-permute-start(f32[2048,128]{1,0:T(8,128)S(1)} %get-tuple-element.37), channel_id=1, source_target_pairs={{0,1},{1,2},{2,3},{3,4},{4,5},{5,6},{6,7},{7,8},{8,9},{9,10},{10,1... | collective-permute-start | bytes 3145736 | tf_op jit(solution)/shard_map/ppermute | solution.py:482
  44.7 23.4 %collective-permute-start.4 = (f32[2048,128]{1,0:T(8,128)S(1)}, f32[2048,128]{1,0:T(8,128)S(1)}, u32[]{:S(2)}, u32[]{:S(2)}) collective-permute-start(f32[2048,128]{1,0:T(8,128)S(1)} %get-tuple-element.42), channel_id=1, source_target_pairs={{0,1},{1,2},{2,3},{3,4},{4,5},{5,6},{6,7},{7,8},{8,9},{9,10},{10,1... | collective-permute-start | bytes 3145736 | tf_op jit(solution)/shard_map/ppermute | solution.py:482
  46.7 1.6 %collective-permute-start.8 = (f32[1120,128]{1,0:T(8,128)S(1)}, f32[1120,128]{1,0:T(8,128)S(1)}, u32[]{:S(2)}, u32[]{:S(2)}) collective-permute-start(f32[1120,128]{1,0:T(8,128)S(1)} %get-tuple-element.51), channel_id=1, source_target_pairs={{32,63},{33,32},{34,33},{35,34},{36,35},{37,36},{38,37},{39,38},{4... | collective-permute-start | bytes 1720328 | tf_op jit(solution)/shard_map/ppermute | solution.py:482
  47.6 25.3 %collective-permute-start.11 = (f32[1024,128]{1,0:T(8,128)S(1)}, f32[1024,128]{1,0:T(8,128)S(1)}, u32[]{:S(2)}, u32[]{:S(2)}) collective-permute-start(f32[1024,128]{1,0:T(8,128)S(1)} %get-tuple-element.56), channel_id=1, source_target_pairs={{32,63},{33,32},{34,33},{35,34},{36,35},{37,36},{38,37},{39,38},{4... | collective-permute-start | bytes 1572872 | tf_op jit(solution)/shard_map/ppermute | solution.py:482
  48.4 26.0 %collective-permute-start.10 = (f32[2048,128]{1,0:T(8,128)S(1)}, f32[2048,128]{1,0:T(8,128)S(1)}, u32[]{:S(2)}, u32[]{:S(2)}) collective-permute-start(f32[2048,128]{1,0:T(8,128)S(1)} %get-tuple-element.55), channel_id=1, source_target_pairs={{32,99},{33,100},{34,101},{35,102},{36,103},{37,104},{38,105},{39,... | collective-permute-start | bytes 3145736 | tf_op jit(solution)/shard_map/ppermute | solution.py:482
  58.6 27.5 %collective-permute-start.3 = (f32[2048,128]{1,0:T(8,128)S(1)}, f32[2048,128]{1,0:T(8,128)S(1)}, u32[]{:S(2)}, u32[]{:S(2)}) collective-permute-start(f32[2048,128]{1,0:T(8,128)S(1)} %get-tuple-element.41), channel_id=1, source_target_pairs={{0,1},{1,2},{2,3},{3,4},{4,5},{5,6},{6,7},{7,8},{8,9},{9,10},{10,1... | collective-permute-start | bytes 3145736 | tf_op jit(solution)/shard_map/ppermute | solution.py:482
  70.9 35.5 %collective-permute-start.13 = (f32[2048,128]{1,0:T(8,128)S(1)}, f32[2048,128]{1,0:T(8,128)S(1)}, u32[]{:S(2)}, u32[]{:S(2)}) collective-permute-start(f32[2048,128]{1,0:T(8,128)S(1)} %get-tuple-element.60), channel_id=1, source_target_pairs={{0,1},{1,2},{2,3},{3,4},{4,5},{5,6},{6,7},{7,8},{8,9},{9,10},{10,1... | collective-permute-start | bytes 3145736 | tf_op jit(solution)/shard_map/ppermute | solution.py:482
  73.0 14.9 %collective-permute-start.15 = (f32[1024,128]{1,0:T(8,128)S(1)}, f32[1024,128]{1,0:T(8,128)S(1)}, u32[]{:S(2)}, u32[]{:S(2)}) collective-permute-start(f32[1024,128]{1,0:T(8,128)S(1)} %get-tuple-element.63), channel_id=1, source_target_pairs={{32,35},{33,36},{34,37},{35,38},{36,39},{37,40},{38,41},{39,42},{4... | collective-permute-start | bytes 1572872 | tf_op jit(solution)/shard_map/ppermute | solution.py:482
  73.7 14.2 %collective-permute-start.14 = (f32[1024,128]{1,0:T(8,128)S(1)}, f32[1024,128]{1,0:T(8,128)S(1)}, u32[]{:S(2)}, u32[]{:S(2)}) collective-permute-start(f32[1024,128]{1,0:T(8,128)S(1)} %get-tuple-element.62), channel_id=1, source_target_pairs={{32,35},{33,36},{34,37},{35,38},{36,39},{37,40},{38,41},{39,42},{4... | collective-permute-start | bytes 1572872 | tf_op jit(solution)/shard_map/ppermute | solution.py:482
  74.4 53.3 %collective-permute-start.17 = (f32[2056,128]{1,0:T(8,128)S(1)}, f32[2056,128]{1,0:T(8,128)S(1)}, u32[]{:S(2)}, u32[]{:S(2)}) collective-permute-start(f32[2056,128]{1,0:T(8,128)S(1)} %get-tuple-element.58.refs_4_), channel_id=1, source_target_pairs={{32,67},{33,68},{34,69},{35,70},{36,71},{37,72},{38,73},{39,74},{4... | collective-permute-start | bytes 3158024 | tf_op jit(solution)/shard_map/ppermute | solution.py:482
  108.3 19.4 %collective-permute-start.16 = (f32[2048,128]{1,0:T(8,128)S(1)}, f32[2048,128]{1,0:T(8,128)S(1)}, u32[]{:S(2)}, u32[]{:S(2)}) collective-permute-start(f32[2048,128]{1,0:T(8,128)S(1)} %get-tuple-element.64), channel_id=1, source_target_pairs={{0,32},{1,33},{2,34},{3,35},{4,36},{5,37},{6,38},{7,39},{8,40},{9,... | collective-permute-start | bytes 3145736 | tf_op jit(solution)/shard_map/ppermute | solution.py:482
  119.0 8.7 %collective-permute-start.12 = (f32[2048,128]{1,0:T(8,128)S(1)}, f32[2048,128]{1,0:T(8,128)S(1)}, u32[]{:S(2)}, u32[]{:S(2)}) collective-permute-start(f32[2048,128]{1,0:T(8,128)S(1)} %get-tuple-element.59), channel_id=1, source_target_pairs={{0,32},{1,33},{2,34},{3,35},{4,36},{5,37},{6,38},{7,39},{8,40},{9,... | collective-permute-start | bytes 3145736 | tf_op jit(solution)/shard_map/ppermute | solution.py:496

commit v2 on v1

--- a/solution.py
+++ b/solution.py
@@ -443,7 +443,7 @@
         waited(heads)
         copies = []
         for n in range(VERT_TILES):
-            source = first if n < SLOTS else late
+            source = second if n < SLOTS else late
             rows = pl.ds(n % SLOTS * TILE, TILE)
             copies.append((source.at[rows], vertex.at[tile(head(spots, n))]))
         waited(moved(copies, sems, 2))
@@ -489,7 +489,7 @@
         x, total = even_step(s, h, e[h], c_state, total, own, give, after)
         if s + 1 < steps:
             e[h] = sent(x, 0, (0, 1))
-        elif h:
+        elif give is None:
             e[h] = sent(x, 0, (1, 0))
         else:
             swap = route(groups, members, 0, (1, 0)) + route(groups, members, 1, (-1, 0))
@@ -514,9 +514,9 @@
     total, early = odd_half(3, 0, None)
     early = sent(early, 1, beside)
     (late,) = odd_half(3, 1, total)
-    total = even_half(3, 0, None, early, late)
+    total = even_half(3, 0, None, None, late)
     late = sent(late, 1, (1, steps - 1))
-    c_state = even_half(3, 1, total, None, *o)
+    c_state = even_half(3, 1, total, early, *o)
     return tuple(finish(*e, late, c_state, *o))
 
 

time: 131 us -> 130 us (level)
  starting transfers between devices: 31.3 us -> 47.1 us
  waiting for transfers between devices: 73.4 us -> 57.7 us
    ppermute x17, waiting for transfers between devices: 73.4 us -> 57.7 us  [sent(): return lax.ppermute(array, AXES, route(groups, members, odd, move))]
    ppermute x17, starting transfers between devices: 31.2 us -> 46.1 us  [sent(): return lax.ppermute(array, AXES, route(groups, members, odd, move))]
    pallas_call x1, Pallas kernels: 6.75 us -> 4.9 us  [first_step(): pl.pallas_call(kernel, out_shape=[wide(HALF), wide(HALF), wide(QUARTER +...]
  transfers between devices with their start and end apart: 18 -> 18, of which waited for: 7 -> 6; matrix products, arithmetic and copies ran while one was open for 0% -> 0% of each run, Pallas kernels for 11% -> 11%
where the time goes in v2:
time: 130 us; the launch traced here: 129 us
  waiting for transfers between devices  57.7 us (44%)
  starting transfers between devices  47.1 us (36%)
  Pallas kernels  21.6 us (17%)
  local copies, waits for them, and re-layouts  1.59 us (1%)
    ppermute x17, waiting for transfers between devices, sent(): return lax.ppermute(array, AXES, route(groups, members, odd, move))  57.7 us
    ppermute x17, starting transfers between devices, sent(): return lax.ppermute(array, AXES, route(groups, members, odd, move))  46.1 us
    pallas_call x6, Pallas kernels, even_step(): pl.pallas_call(kernel, out_shape=[wide(size), wide(HALF)], in_specs=[ANY]...  13.9 us
    pallas_call x1, Pallas kernels, first_step(): pl.pallas_call(kernel, out_shape=[wide(HALF), wide(HALF), wide(QUARTER +...  4.9 us
  transfers between devices with their start and end apart: 18, of which 6 were waited for; matrix products, arithmetic and copies ran while one was open for 0% of the time, Pallas kernels for 11%

profile of v2, /device:TPU:0, one launch (start us, length us, event | category | flops | bytes accessed | tf_op | source)
XLA Modules:
  0.0 129.1 jit_solution(10269565494723008088)
XLA Ops:
  0.6 4.9 %shard_map.86 = (f32[2048,128]{1,0:T(8,128)}, f32[2048,128]{1,0:T(8,128)}, f32[1312,128]{1,0:T(8,128)}, f32[1024,128]{1,0:T(8,128)}, f32[2048,128]{1,0:T(8,128)}...) custom-call(f32[4096,128]{1,0:T(8,128)} %refs_0_.1, f32[2048,128]{1,0:T(8,128)} %refs_1_.1, s32[4]{0:T(128)} %refs_2_.1, ...), custom_call_target="tpu_custom_call" | custom-call | flops 1000 | bytes 1000 | tf_op jit(solution)/shard_map/pallas_call | solution.py:209
  5.5 0.7 collective-permute-start.6
  6.3 4.4 %collective-permute-start = (f32[2048,128]{1,0:T(8,128)}, f32[2048,128]{1,0:T(8,128)S(1)}, u32[]{:S(2)}, u32[]{:S(2)}) collective-permute-start(f32[2048,128]{1,0:T(8,128)} %get-tuple-element.34), channel_id=1, source_target_pairs={{0,1},{1,2},{2,3},{3,4},{4,5},{5,6},{6,7},{7,8},{8,9},{9,10},{10,1... | collective-permute-start | bytes 3145736 | tf_op jit(solution)/shard_map/ppermute | solution.py:482
  10.7 4.3 %collective-permute-start.2 = (f32[2048,128]{1,0:T(8,128)}, f32[2048,128]{1,0:T(8,128)S(1)}, u32[]{:S(2)}, u32[]{:S(2)}) collective-permute-start(f32[2048,128]{1,0:T(8,128)} %get-tuple-element.38), channel_id=1, source_target_pairs={{0,1},{1,2},{2,3},{3,4},{4,5},{5,6},{6,7},{7,8},{8,9},{9,10},{10,1... | collective-permute-start | bytes 3145736 | tf_op jit(solution)/shard_map/ppermute | solution.py:482
  15.0 0.7 collective-permute-start.5
  15.7 1.6 %copy-done.2 = f32[4096,128]{1,0:T(8,128)S(1)} copy-done((f32[4096,128]{1,0:T(8,128)S(1)}, f32[4096,128]{1,0:T(8,128)}, u32[]{:S(2)}) %copy-start.2) | copy-done | bytes 2097176
  17.4 0.8 collective-permute-start.8
  18.3 13.3 %collective-permute-done.refs_0_ = f32[2048,128]{1,0:T(8,128)S(1)} collective-permute-done((f32[2048,128]{1,0:T(8,128)}, f32[2048,128]{1,0:T(8,128)S(1)}, u32[]{:S(2)}, u32[]{:S(2)}) %collective-permute-start) | collective-permute-done | bytes 1048608 | tf_op jit(solution)/shard_map/ppermute | solution.py:482
  31.6 0.9 shard_map.87
  32.5 1.9 %collective-permute-start.1 = (f32[2048,128]{1,0:T(8,128)S(1)}, f32[2048,128]{1,0:T(8,128)S(1)}, u32[]{:S(2)}, u32[]{:S(2)}) collective-permute-start(f32[2048,128]{1,0:T(8,128)S(1)} %get-tuple-element.37), channel_id=1, source_target_pairs={{0,1},{1,2},{2,3},{3,4},{4,5},{5,6},{6,7},{7,8},{8,9},{9,10},{10,1... | collective-permute-start | bytes 3145736 | tf_op jit(solution)/shard_map/ppermute | solution.py:482
  34.6 0.7 collective-permute-start.7
  35.3 7.6 %collective-permute-done.2.refs_0_ = f32[2048,128]{1,0:T(8,128)S(1)} collective-permute-done((f32[2048,128]{1,0:T(8,128)}, f32[2048,128]{1,0:T(8,128)S(1)}, u32[]{:S(2)}, u32[]{:S(2)}) %collective-permute-start.2) | collective-permute-done | bytes 1048608 | tf_op jit(solution)/shard_map/ppermute | solution.py:482
  42.8 1.8 %shard_map.88 = (f32[2048,128]{1,0:T(8,128)S(1)}, f32[2048,128]{1,0:T(8,128)S(1)}) custom-call(f32[2048,128]{1,0:T(8,128)S(1)} %collective-permute-done.2.refs_0_, f32[2048,128]{1,0:T(8,128)S(1)} %copy-done.1, f32[2048,128]{1,0:T(8,128)S(1)} %get-tuple-element.39.refs_2_, f32[288,128]{1,0:T(8,128)S(1)} %copy-done), custom_call_target="tpu_custom_call" | custom-call | flops 1000 | bytes 1000 | tf_op jit(solution)/shard_map/pallas_call | solution.py:305
  44.7 1.9 %collective-permute-start.4 = (f32[2048,128]{1,0:T(8,128)S(1)}, f32[2048,128]{1,0:T(8,128)S(1)}, u32[]{:S(2)}, u32[]{:S(2)}) collective-permute-start(f32[2048,128]{1,0:T(8,128)S(1)} %get-tuple-element.42), channel_id=1, source_target_pairs={{0,1},{1,2},{2,3},{3,4},{4,5},{5,6},{6,7},{7,8},{8,9},{9,10},{10,1... | collective-permute-start | bytes 3145736 | tf_op jit(solution)/shard_map/ppermute | solution.py:482
  46.7 0.7 collective-permute-start.10
  47.6 0.7 collective-permute-start.9
  48.3 6.6 %collective-permute-done.1.refs_0_ = f32[2048,128]{1,0:T(8,128)S(1)} collective-permute-done((f32[2048,128]{1,0:T(8,128)S(1)}, f32[2048,128]{1,0:T(8,128)S(1)}, u32[]{:S(2)}, u32[]{:S(2)}) %collective-permute-start.1) | collective-permute-done | bytes 1048608 | tf_op jit(solution)/shard_map/ppermute | solution.py:482
  54.9 3.7 %shard_map.89 = (f32[2048,128]{1,0:T(8,128)S(1)}, f32[2048,128]{1,0:T(8,128)S(1)}) custom-call(f32[2048,128]{1,0:T(8,128)S(1)} %collective-permute-done.1.refs_0_, f32[2048,128]{1,0:T(8,128)S(1)} %get-tuple-element.40.refs_1_, f32[288,128]{1,0:T(8,128)S(1)} %copy-done), custom_call_target="tpu_custom_call" | custom-call | flops 1000 | bytes 1000 | tf_op jit(solution)/shard_map/pallas_call | solution.py:305
  58.6 1.9 %collective-permute-start.3 = (f32[2048,128]{1,0:T(8,128)S(1)}, f32[2048,128]{1,0:T(8,128)S(1)}, u32[]{:S(2)}, u32[]{:S(2)}) collective-permute-start(f32[2048,128]{1,0:T(8,128)S(1)} %get-tuple-element.41), channel_id=1, source_target_pairs={{0,1},{1,2},{2,3},{3,4},{4,5},{5,6},{6,7},{7,8},{8,9},{9,10},{10,1... | collective-permute-start | bytes 3145736 | tf_op jit(solution)/shard_map/ppermute | solution.py:482
  60.7 0.7 collective-permute-start.13
  61.4 5.7 %collective-permute-done.4.refs_0_ = f32[2048,128]{1,0:T(8,128)S(1)} collective-permute-done((f32[2048,128]{1,0:T(8,128)S(1)}, f32[2048,128]{1,0:T(8,128)S(1)}, u32[]{:S(2)}, u32[]{:S(2)}) %collective-permute-start.4) | collective-permute-done | bytes 1048608 | tf_op jit(solution)/shard_map/ppermute | solution.py:482
  67.1 2.0 %shard_map.90 = (f32[2048,128]{1,0:T(8,128)S(1)}, f32[2048,128]{1,0:T(8,128)S(1)}) custom-call(f32[2048,128]{1,0:T(8,128)S(1)} %collective-permute-done.4.refs_0_, f32[2048,128]{1,0:T(8,128)S(1)} %get-tuple-element.40.refs_1_, f32[2048,128]{1,0:T(8,128)S(1)} %get-tuple-element.43.refs_2_, f32[288,128]{1,0:T(8,128)S(1)} %copy-done), custom_call_target="tpu_custom_call" | custom-call | flops 1000 | bytes 1000 | tf_op jit(solution)/shard_map/pallas_call | solution.py:305
  69.1 1.9 %collective-permute-start.12 = (f32[2048,128]{1,0:T(8,128)S(1)}, f32[2048,128]{1,0:T(8,128)S(1)}, u32[]{:S(2)}, u32[]{:S(2)}) collective-permute-start(f32[2048,128]{1,0:T(8,128)S(1)} %get-tuple-element.59), channel_id=1, source_target_pairs={{0,1},{1,2},{2,3},{3,4},{4,5},{5,6},{6,7},{7,8},{8,9},{9,10},{10,1... | collective-permute-start | bytes 3145736 | tf_op jit(solution)/shard_map/ppermute | solution.py:482
  71.1 0.7 collective-permute-start.15
  72.6 12.3 %collective-permute-done.3.refs_0_ = f32[2048,128]{1,0:T(8,128)S(1)} collective-permute-done((f32[2048,128]{1,0:T(8,128)S(1)}, f32[2048,128]{1,0:T(8,128)S(1)}, u32[]{:S(2)}, u32[]{:S(2)}) %collective-permute-start.3) | collective-permute-done | bytes 1048608 | tf_op jit(solution)/shard_map/ppermute | solution.py:482
  84.9 1.3 collective-permute-start.17
  86.1 2.8 %shard_map.97 = (f32[2048,128]{1,0:T(8,128)S(1)}, f32[2048,128]{1,0:T(8,128)S(1)}) custom-call(f32[2048,128]{1,0:T(8,128)S(1)} %collective-permute-done.3.refs_0_, f32[2048,128]{1,0:T(8,128)S(1)} %get-tuple-element.44.refs_1_, f32[288,128]{1,0:T(8,128)S(1)} %copy-done, f32[2056,128]{1,0:T(8,128)S(1)} %get-tuple-element.57.refs_3_), custom_call_target="tpu_custom_call" | custom-call | flops 1000 | bytes 1000 | tf_op jit(solution)/shard_map/pallas_call | solution.py:305
  88.9 22.0 %collective-permute-start.11 = (f32[2048,128]{1,0:T(8,128)S(1)}, f32[2048,128]{1,0:T(8,128)S(1)}, u32[]{:S(2)}, u32[]{:S(2)}) collective-permute-start(f32[2048,128]{1,0:T(8,128)S(1)} %get-tuple-element.58), channel_id=1, source_target_pairs={{0,32},{1,33},{2,34},{3,35},{4,36},{5,37},{6,38},{7,39},{8,40},{9,... | collective-permute-start | bytes 3145736 | tf_op jit(solution)/shard_map/ppermute | solution.py:482
  110.9 2.8 %shard_map.98 = (f32[2048,128]{1,0:T(8,128)S(1)}, f32[2048,128]{1,0:T(8,128)S(1)}) custom-call(f32[2048,128]{1,0:T(8,128)S(1)} %collective-permute-done.12.refs_0_, f32[2048,128]{1,0:T(8,128)S(1)} %get-tuple-element.44.refs_1_, f32[2048,128]{1,0:T(8,128)S(1)} %get-tuple-element.60.refs_2_, f32[288,128]{1,0:T(8,128)S(1)} %copy-done, ...), custom_call_target="tpu_custom_call" | custom-call | flops 1000 | bytes 1000 | tf_op jit(solution)/shard_map/pallas_call | solution.py:305
  113.7 1.1 collective-permute-start.16
  114.8 12.1 %collective-permute-done.17.late = f32[2056,128]{1,0:T(8,128)S(1)} collective-permute-done((f32[2056,128]{1,0:T(8,128)S(1)}, f32[2056,128]{1,0:T(8,128)S(1)}, u32[]{:S(2)}, u32[]{:S(2)}) %collective-permute-start.17) | collective-permute-done | bytes 1052704 | tf_op jit(solution)/shard_map/ppermute | solution.py:482
  126.9 2.1 %shard_map.99 = (f32[4096,128]{1,0:T(8,128)}, f32[2048,128]{1,0:T(8,128)}) custom-call(f32[2048,128]{1,0:T(8,128)S(1)} %collective-permute-done.11.first, f32[2048,128]{1,0:T(8,128)S(1)} %collective-permute-done.16.second, f32[2056,128]{1,0:T(8,128)S(1)} %collective-permute-done.17.late, f32[2048,128]{1,0:T(8,128)S(1)} %get-tuple-element.65.stayed, ...), custom_call_target="tpu_custom_call" | custom-call | tf_op jit(solution)/shard_map/pallas_call | solution.py:464
  (24 shorter events, 1.5 us)
Async XLA Ops:
  5.5 10.2 %collective-permute-start.6 = (f32[1312,128]{1,0:T(8,128)}, f32[1312,128]{1,0:T(8,128)S(1)}, u32[]{:S(2)}, u32[]{:S(2)}) collective-permute-start(f32[1312,128]{1,0:T(8,128)} %get-tuple-element.47), channel_id=1, source_target_pairs={{32,63},{33,32},{34,33},{35,34},{36,35},{37,36},{38,37},{39,38},{4... | collective-permute-start | bytes 2015240 | tf_op jit(solution)/shard_map/ppermute | solution.py:482
  6.3 25.3 %collective-permute-start = (f32[2048,128]{1,0:T(8,128)}, f32[2048,128]{1,0:T(8,128)S(1)}, u32[]{:S(2)}, u32[]{:S(2)}) collective-permute-start(f32[2048,128]{1,0:T(8,128)} %get-tuple-element.34), channel_id=1, source_target_pairs={{0,1},{1,2},{2,3},{3,4},{4,5},{5,6},{6,7},{7,8},{8,9},{9,10},{10,1... | collective-permute-start | bytes 3145736 | tf_op jit(solution)/shard_map/ppermute | solution.py:482
  10.7 32.2 %collective-permute-start.2 = (f32[2048,128]{1,0:T(8,128)}, f32[2048,128]{1,0:T(8,128)S(1)}, u32[]{:S(2)}, u32[]{:S(2)}) collective-permute-start(f32[2048,128]{1,0:T(8,128)} %get-tuple-element.38), channel_id=1, source_target_pairs={{0,1},{1,2},{2,3},{3,4},{4,5},{5,6},{6,7},{7,8},{8,9},{9,10},{10,1... | collective-permute-start | bytes 3145736 | tf_op jit(solution)/shard_map/ppermute | solution.py:482
  15.0 19.4 %collective-permute-start.5 = (f32[1024,128]{1,0:T(8,128)}, f32[1024,128]{1,0:T(8,128)S(1)}, u32[]{:S(2)}, u32[]{:S(2)}) collective-permute-start(f32[1024,128]{1,0:T(8,128)} %get-tuple-element.45), channel_id=1, source_target_pairs={{32,63},{33,32},{34,33},{35,34},{36,35},{37,36},{38,37},{39,38},{4... | collective-permute-start | bytes 1572872 | tf_op jit(solution)/shard_map/ppermute | solution.py:482
  15.7 1.6 %copy-start.2 = (f32[4096,128]{1,0:T(8,128)S(1)}, f32[4096,128]{1,0:T(8,128)}, u32[]{:S(2)}) copy-start(f32[4096,128]{1,0:T(8,128)} %get-tuple-element.46.refs_1_) | copy-start | bytes 6291460
  17.3 14.3 %copy-start = (f32[288,128]{1,0:T(8,128)S(1)}, f32[288,128]{1,0:T(8,128)}, u32[]{:S(2)}) copy-start(f32[288,128]{1,0:T(8,128)} %get-tuple-element.36.refs_2_.refs_3_) | copy-start | bytes 442372
  17.3 14.3 %copy-start.1 = (f32[2048,128]{1,0:T(8,128)S(1)}, f32[2048,128]{1,0:T(8,128)}, u32[]{:S(2)}) copy-start(f32[2048,128]{1,0:T(8,128)} %get-tuple-element.35.refs_1_) | copy-start | bytes 3145732
  17.4 29.2 %collective-permute-start.8 = (f32[1216,128]{1,0:T(8,128)S(1)}, f32[1216,128]{1,0:T(8,128)S(1)}, u32[]{:S(2)}, u32[]{:S(2)}) collective-permute-start(f32[1216,128]{1,0:T(8,128)S(1)} %get-tuple-element.51), channel_id=1, source_target_pairs={{32,63},{33,32},{34,33},{35,34},{36,35},{37,36},{38,37},{39,38},{4... | collective-permute-start | bytes 1867784 | tf_op jit(solution)/shard_map/ppermute | solution.py:482
  32.5 22.4 %collective-permute-start.1 = (f32[2048,128]{1,0:T(8,128)S(1)}, f32[2048,128]{1,0:T(8,128)S(1)}, u32[]{:S(2)}, u32[]{:S(2)}) collective-permute-start(f32[2048,128]{1,0:T(8,128)S(1)} %get-tuple-element.37), channel_id=1, source_target_pairs={{0,1},{1,2},{2,3},{3,4},{4,5},{5,6},{6,7},{7,8},{8,9},{9,10},{10,1... | collective-permute-start | bytes 3145736 | tf_op jit(solution)/shard_map/ppermute | solution.py:482
  34.6 12.9 %collective-permute-start.7 = (f32[1024,128]{1,0:T(8,128)S(1)}, f32[1024,128]{1,0:T(8,128)S(1)}, u32[]{:S(2)}, u32[]{:S(2)}) collective-permute-start(f32[1024,128]{1,0:T(8,128)S(1)} %get-tuple-element.49), channel_id=1, source_target_pairs={{32,63},{33,32},{34,33},{35,34},{36,35},{37,36},{38,37},{39,38},{4... | collective-permute-start | bytes 1572872 | tf_op jit(solution)/shard_map/ppermute | solution.py:482
  44.7 22.4 %collective-permute-start.4 = (f32[2048,128]{1,0:T(8,128)S(1)}, f32[2048,128]{1,0:T(8,128)S(1)}, u32[]{:S(2)}, u32[]{:S(2)}) collective-permute-start(f32[2048,128]{1,0:T(8,128)S(1)} %get-tuple-element.42), channel_id=1, source_target_pairs={{0,1},{1,2},{2,3},{3,4},{4,5},{5,6},{6,7},{7,8},{8,9},{9,10},{10,1... | collective-permute-start | bytes 3145736 | tf_op jit(solution)/shard_map/ppermute | solution.py:482
  46.7 13.8 %collective-permute-start.10 = (f32[1120,128]{1,0:T(8,128)S(1)}, f32[1120,128]{1,0:T(8,128)S(1)}, u32[]{:S(2)}, u32[]{:S(2)}) collective-permute-start(f32[1120,128]{1,0:T(8,128)S(1)} %get-tuple-element.55), channel_id=1, source_target_pairs={{32,63},{33,32},{34,33},{35,34},{36,35},{37,36},{38,37},{39,38},{4... | collective-permute-start | bytes 1720328 | tf_op jit(solution)/shard_map/ppermute | solution.py:482
  47.6 23.4 %collective-permute-start.9 = (f32[1024,128]{1,0:T(8,128)S(1)}, f32[1024,128]{1,0:T(8,128)S(1)}, u32[]{:S(2)}, u32[]{:S(2)}) collective-permute-start(f32[1024,128]{1,0:T(8,128)S(1)} %get-tuple-element.53), channel_id=1, source_target_pairs={{32,63},{33,32},{34,33},{35,34},{36,35},{37,36},{38,37},{39,38},{4... | collective-permute-start | bytes 1572872 | tf_op jit(solution)/shard_map/ppermute | solution.py:482
  58.6 26.3 %collective-permute-start.3 = (f32[2048,128]{1,0:T(8,128)S(1)}, f32[2048,128]{1,0:T(8,128)S(1)}, u32[]{:S(2)}, u32[]{:S(2)}) collective-permute-start(f32[2048,128]{1,0:T(8,128)S(1)} %get-tuple-element.41), channel_id=1, source_target_pairs={{0,1},{1,2},{2,3},{3,4},{4,5},{5,6},{6,7},{7,8},{8,9},{9,10},{10,1... | collective-permute-start | bytes 3145736 | tf_op jit(solution)/shard_map/ppermute | solution.py:482
  60.7 50.2 %collective-permute-start.13 = (f32[2048,128]{1,0:T(8,128)S(1)}, f32[2048,128]{1,0:T(8,128)S(1)}, u32[]{:S(2)}, u32[]{:S(2)}) collective-permute-start(f32[2048,128]{1,0:T(8,128)S(1)} %get-tuple-element.61), channel_id=1, source_target_pairs={{32,99},{33,100},{34,101},{35,102},{36,103},{37,104},{38,105},{39,... | collective-permute-start | bytes 3145736 | tf_op jit(solution)/shard_map/ppermute | solution.py:482
  69.1 41.8 %collective-permute-start.12 = (f32[2048,128]{1,0:T(8,128)S(1)}, f32[2048,128]{1,0:T(8,128)S(1)}, u32[]{:S(2)}, u32[]{:S(2)}) collective-permute-start(f32[2048,128]{1,0:T(8,128)S(1)} %get-tuple-element.59), channel_id=1, source_target_pairs={{0,1},{1,2},{2,3},{3,4},{4,5},{5,6},{6,7},{7,8},{8,9},{9,10},{10,1... | collective-permute-start | bytes 3145736 | tf_op jit(solution)/shard_map/ppermute | solution.py:482
  71.1 17.8 %collective-permute-start.15 = (f32[1024,128]{1,0:T(8,128)S(1)}, f32[1024,128]{1,0:T(8,128)S(1)}, u32[]{:S(2)}, u32[]{:S(2)}) collective-permute-start(f32[1024,128]{1,0:T(8,128)S(1)} %get-tuple-element.63), channel_id=1, source_target_pairs={{32,35},{33,36},{34,37},{35,38},{36,39},{37,40},{38,41},{39,42},{4... | collective-permute-start | bytes 1572872 | tf_op jit(solution)/shard_map/ppermute | solution.py:482
  71.8 39.0 %collective-permute-start.14 = (f32[1024,128]{1,0:T(8,128)S(1)}, f32[1024,128]{1,0:T(8,128)S(1)}, u32[]{:S(2)}, u32[]{:S(2)}) collective-permute-start(f32[1024,128]{1,0:T(8,128)S(1)} %get-tuple-element.62), channel_id=1, source_target_pairs={{32,35},{33,36},{34,37},{35,38},{36,39},{37,40},{38,41},{39,42},{4... | collective-permute-start | bytes 1572872 | tf_op jit(solution)/shard_map/ppermute | solution.py:482
  84.9 42.1 %collective-permute-start.17 = (f32[2056,128]{1,0:T(8,128)S(1)}, f32[2056,128]{1,0:T(8,128)S(1)}, u32[]{:S(2)}, u32[]{:S(2)}) collective-permute-start(f32[2056,128]{1,0:T(8,128)S(1)} %get-tuple-element.57.refs_3_), channel_id=1, source_target_pairs={{32,67},{33,68},{34,69},{35,70},{36,71},{37,72},{38,73},{39,74},{4... | collective-permute-start | bytes 3158024 | tf_op jit(solution)/shard_map/ppermute | solution.py:482
  88.9 38.0 %collective-permute-start.11 = (f32[2048,128]{1,0:T(8,128)S(1)}, f32[2048,128]{1,0:T(8,128)S(1)}, u32[]{:S(2)}, u32[]{:S(2)}) collective-permute-start(f32[2048,128]{1,0:T(8,128)S(1)} %get-tuple-element.58), channel_id=1, source_target_pairs={{0,32},{1,33},{2,34},{3,35},{4,36},{5,37},{6,38},{7,39},{8,40},{9,... | collective-permute-start | bytes 3145736 | tf_op jit(solution)/shard_map/ppermute | solution.py:482
  113.7 13.2 %collective-permute-start.16 = (f32[2048,128]{1,0:T(8,128)S(1)}, f32[2048,128]{1,0:T(8,128)S(1)}, u32[]{:S(2)}, u32[]{:S(2)}) collective-permute-start(f32[2048,128]{1,0:T(8,128)S(1)} %get-tuple-element.64), channel_id=1, source_target_pairs={{0,32},{1,33},{2,34},{3,35},{4,36},{5,37},{6,38},{7,39},{8,40},{9,... | collective-permute-start | bytes 3145736 | tf_op jit(solution)/shard_map/ppermute | solution.py:496

commit v3 on v2

--- a/solution.py
+++ b/solution.py
@@ -343,6 +343,9 @@
     if half:
         carrier, total_in, *refs = refs
         list_in = carrier.at[pl.ds(QUARTER, LISTED)]
+    joins = half and left == 0
+    if joins:
+        low_half, *refs = refs
     refs = refs[n_after:]
     move_out, *refs = refs
     if left or not half:
@@ -364,6 +367,8 @@
         if left and not half:
             rest = pl.ds(QUARTER, LISTED * left)
             loads.append((move_in.at[pl.ds(QUARTER + LISTED, LISTED * left)], move_out.at[rest]))
+        if joins:
+            loads.append((low_half, move_out.at[pl.ds(0, QUARTER)]))
         loads = moved(loads, sems, 2)
         waited(heads)
         mine = choose(chosen, head(meta, 16), lambda t: head(meta, 8 + t) // 4 == half)
@@ -378,7 +383,7 @@
             return s_new, vi, dv, m_new, ci, dc
 
         run_pairs(chosen, mine, one)
-        stores = [(m_new, move_out.at[pl.ds(0, QUARTER)])]
+        stores = [(m_new, move_out.at[pl.ds(QUARTER if joins else 0, QUARTER)])]
         if left or not half:
             stores.append((s_new, stay_out))
         if parts:
@@ -394,16 +399,20 @@
                 spot = jnp.where(lane == n, order[n], spot)
             places[...] = spot.astype(jnp.float32)
             stores.append((places, part_out.at[pl.ds(HALF, 8)]))
+            stores.append((places, move_out.at[pl.ds(HALF, 8)]))
         waited(moved(stores, sems))
 
 
-def odd_step(left, half, moving, staying, carrier, total, after):
+def odd_step(left, half, moving, staying, carrier, total, low, after):
     operands = [moving, staying]
-    out_shape = [wide(QUARTER + (0 if half else LISTED * left))]
+    joins = half and left == 0
+    out_shape = [wide(HALF + 8 if joins else QUARTER + (0 if half else LISTED * left))]
     if left or not half:
         out_shape.append(wide(2 * HALF))
     if half:
         operands += [carrier, total]
+    if joins:
+        operands.append(low)
     if left == 0:
         out_shape.append(wide(HALF + 8 if half else HALF))
 
@@ -426,14 +435,14 @@
             pltpu.SMEM((VERT_TILES,), jnp.int32),
             pltpu.SMEM((VERT_TILES,), jnp.int32),
             vmem(8),
-            pltpu.SemaphoreType.DMA((12,)),
+            pltpu.SemaphoreType.DMA((13,)),
         ],
         compiler_params=pltpu.CompilerParams(vmem_limit_bytes=STEP_LIMIT),
-        cost_estimate=pl.CostEstimate(flops=4000000000, bytes_accessed=1000, transcendentals=0),
+        cost_estimate=pl.CostEstimate(flops=16000000000, bytes_accessed=1000, transcendentals=0),
     )(*operands, *after)
 
 
-def finish_kernel(first, second, late, stayed, home, home_high, vertex, context, spots, sems):
+def finish_kernel(first, second, late, stayed, home, vertex, context, spots, sems):
     odd = group_odd()
 
     @pl.when(odd == 0)
@@ -454,8 +463,7 @@
         copies = [
             (first, vertex.at[pl.ds(0, HALF)]),
             (second, vertex.at[pl.ds(HALF, HALF)]),
-            (home, context.at[pl.ds(0, QUARTER)]),
-            (home_high, context.at[pl.ds(QUARTER, QUARTER)]),
+            (home.at[pl.ds(0, HALF)], context),
         ]
         waited(moved(copies, sems))
 
@@ -464,7 +472,7 @@
     return pl.pallas_call(
         finish_kernel,
         out_shape=[wide(2 * HALF), wide(HALF)],
-        in_specs=[ANY] * 6,
+        in_specs=[ANY] * 5,
         out_specs=[HBM, HBM],
         scratch_shapes=[
             pltpu.SMEM((8, 128), jnp.float32),
@@ -499,8 +507,11 @@
     def odd_half(s, h, total, *after):
         carrier = None if h == 0 else carriers[s]
         carriers[s] = o[h] if h == 0 else carrier
-        x, *rest = odd_step(steps - 1 - s, h, o[h], v_state, carrier, total, after)
-        o[h] = sent(x, 1, (0, -1) if s + 1 < steps else (0, steps - 1))
+        x, *rest = odd_step(steps - 1 - s, h, o[h], v_state, carrier, total, o[0], after)
+        if s + 1 < steps:
+            o[h] = sent(x, 1, (0, -1))
+        else:
+            o[h] = sent(x, 1, (0, steps - 1)) if h else x
         return rest
 
     carriers = {}
@@ -516,8 +527,8 @@
     (late,) = odd_half(3, 1, total)
     total = even_half(3, 0, None, None, late)
     late = sent(late, 1, (1, steps - 1))
-    c_state = even_half(3, 1, total, early, *o)
-    return tuple(finish(*e, late, c_state, *o))
+    c_state = even_half(3, 1, total, early)
+    return tuple(finish(*e, late, c_state, o[1]))
 
 
 def solution(mesh):

time: 130 us -> 128 us (0.985); the launches traced: 129 us -> 129 us
  starting transfers between devices: 47.1 us -> 22.1 us
  waiting for transfers between devices: 57.7 us -> 81.3 us
    ppermute x17 -> x16, starting transfers between devices: 46.1 us -> 22.1 us  [sent(): return lax.ppermute(array, AXES, route(groups, members, odd, move))]
    ppermute x17 -> x16, waiting for transfers between devices: 57.7 us -> 81.2 us  [sent(): return lax.ppermute(array, AXES, route(groups, members, odd, move))]
  transfers between devices with their start and end apart: 18 -> 17, of which waited for: 6 -> 7; matrix products, arithmetic and copies ran while one was open for 0% -> 0% of each run, Pallas kernels for 11% -> 11%
where the time goes in v3:
time: 128 us; the launch traced here: 129 us
  waiting for transfers between devices  81.3 us (64%)
  Pallas kernels  22.6 us (18%)
  starting transfers between devices  22.1 us (17%)
  local copies, waits for them, and re-layouts  1.59 us (1%)
    ppermute x16, waiting for transfers between devices, sent(): return lax.ppermute(array, AXES, route(groups, members, odd, move))  81.2 us
    ppermute x16, starting transfers between devices, sent(): return lax.ppermute(array, AXES, route(groups, members, odd, move))  22.1 us
    pallas_call x6, Pallas kernels, even_step(): pl.pallas_call(kernel, out_shape=[wide(size), wide(HALF)], in_specs=[ANY]...  13.9 us
    pallas_call x1, Pallas kernels, first_step(): pl.pallas_call(kernel, out_shape=[wide(HALF), wide(HALF), wide(QUARTER +...  5.83 us
  transfers between devices with their start and end apart: 17, of which 7 were waited for; matrix products, arithmetic and copies ran while one was open for 0% of the time, Pallas kernels for 11%

profile of v3, /device:TPU:0, one launch (start us, length us, event | category | flops | bytes accessed | tf_op | source)
XLA Modules:
  0.0 128.7 jit_solution(10210677343232222461)
XLA Ops:
  0.6 5.8 %shard_map.86 = (f32[2048,128]{1,0:T(8,128)}, f32[2048,128]{1,0:T(8,128)}, f32[1312,128]{1,0:T(8,128)}, f32[1024,128]{1,0:T(8,128)}, f32[2048,128]{1,0:T(8,128)}...) custom-call(f32[4096,128]{1,0:T(8,128)} %refs_0_.1, f32[2048,128]{1,0:T(8,128)} %refs_1_.1, s32[4]{0:T(128)} %refs_2_.1, ...), custom_call_target="tpu_custom_call" | custom-call | flops 1000 | bytes 1000 | tf_op jit(solution)/shard_map/pallas_call | solution.py:209
  6.5 0.7 collective-permute-start.6
  7.2 0.7 collective-permute-start.5
  7.9 3.5 %collective-permute-start = (f32[2048,128]{1,0:T(8,128)}, f32[2048,128]{1,0:T(8,128)S(1)}, u32[]{:S(2)}, u32[]{:S(2)}) collective-permute-start(f32[2048,128]{1,0:T(8,128)} %get-tuple-element.34), channel_id=1, source_target_pairs={{0,1},{1,2},{2,3},{3,4},{4,5},{5,6},{6,7},{7,8},{8,9},{9,10},{10,1... | collective-permute-start | bytes 3145736 | tf_op jit(solution)/shard_map/ppermute | solution.py:490
  11.4 2.5 %collective-permute-start.2 = (f32[2048,128]{1,0:T(8,128)}, f32[2048,128]{1,0:T(8,128)S(1)}, u32[]{:S(2)}, u32[]{:S(2)}) collective-permute-start(f32[2048,128]{1,0:T(8,128)} %get-tuple-element.38), channel_id=1, source_target_pairs={{0,1},{1,2},{2,3},{3,4},{4,5},{5,6},{6,7},{7,8},{8,9},{9,10},{10,1... | collective-permute-start | bytes 3145736 | tf_op jit(solution)/shard_map/ppermute | solution.py:490
  13.9 1.6 %copy-done.2 = f32[4096,128]{1,0:T(8,128)S(1)} copy-done((f32[4096,128]{1,0:T(8,128)S(1)}, f32[4096,128]{1,0:T(8,128)}, u32[]{:S(2)}) %copy-start.2) | copy-done | bytes 2097176
  15.6 0.7 collective-permute-start.8
  16.5 0.8 collective-permute-start.7
  17.3 15.0 %collective-permute-done.refs_0_ = f32[2048,128]{1,0:T(8,128)S(1)} collective-permute-done((f32[2048,128]{1,0:T(8,128)}, f32[2048,128]{1,0:T(8,128)S(1)}, u32[]{:S(2)}, u32[]{:S(2)}) %collective-permute-start) | collective-permute-done | bytes 1048608 | tf_op jit(solution)/shard_map/ppermute | solution.py:490
  32.3 1.8 %shard_map.87 = (f32[2048,128]{1,0:T(8,128)S(1)}, f32[2048,128]{1,0:T(8,128)S(1)}) custom-call(f32[2048,128]{1,0:T(8,128)S(1)} %collective-permute-done.refs_0_, f32[2048,128]{1,0:T(8,128)S(1)} %copy-done.1, f32[288,128]{1,0:T(8,128)S(1)} %copy-done), custom_call_target="tpu_custom_call" | custom-call | flops 1000 | bytes 1000 | tf_op jit(solution)/shard_map/pallas_call | solution.py:305
  34.1 1.9 %collective-permute-start.1 = (f32[2048,128]{1,0:T(8,128)S(1)}, f32[2048,128]{1,0:T(8,128)S(1)}, u32[]{:S(2)}, u32[]{:S(2)}) collective-permute-start(f32[2048,128]{1,0:T(8,128)S(1)} %get-tuple-element.37), channel_id=1, source_target_pairs={{0,1},{1,2},{2,3},{3,4},{4,5},{5,6},{6,7},{7,8},{8,9},{9,10},{10,1... | collective-permute-start | bytes 3145736 | tf_op jit(solution)/shard_map/ppermute | solution.py:490
  36.1 7.5 %collective-permute-done.2.refs_0_ = f32[2048,128]{1,0:T(8,128)S(1)} collective-permute-done((f32[2048,128]{1,0:T(8,128)}, f32[2048,128]{1,0:T(8,128)S(1)}, u32[]{:S(2)}, u32[]{:S(2)}) %collective-permute-start.2) | collective-permute-done | bytes 1048608 | tf_op jit(solution)/shard_map/ppermute | solution.py:490
  43.5 3.7 %shard_map.88 = (f32[2048,128]{1,0:T(8,128)S(1)}, f32[2048,128]{1,0:T(8,128)S(1)}) custom-call(f32[2048,128]{1,0:T(8,128)S(1)} %collective-permute-done.2.refs_0_, f32[2048,128]{1,0:T(8,128)S(1)} %copy-done.1, f32[2048,128]{1,0:T(8,128)S(1)} %get-tuple-element.39.refs_2_, f32[288,128]{1,0:T(8,128)S(1)} %copy-done), custom_call_target="tpu_custom_call" | custom-call | flops 1000 | bytes 1000 | tf_op jit(solution)/shard_map/pallas_call | solution.py:305
  47.2 1.9 %collective-permute-start.4 = (f32[2048,128]{1,0:T(8,128)S(1)}, f32[2048,128]{1,0:T(8,128)S(1)}, u32[]{:S(2)}, u32[]{:S(2)}) collective-permute-start(f32[2048,128]{1,0:T(8,128)S(1)} %get-tuple-element.42), channel_id=1, source_target_pairs={{0,1},{1,2},{2,3},{3,4},{4,5},{5,6},{6,7},{7,8},{8,9},{9,10},{10,1... | collective-permute-start | bytes 3145736 | tf_op jit(solution)/shard_map/ppermute | solution.py:490
  49.3 0.7 collective-permute-start.10
  50.2 0.7 collective-permute-start.9
  51.0 0.7 collective-permute-start.13
  51.8 4.8 %collective-permute-done.1.refs_0_ = f32[2048,128]{1,0:T(8,128)S(1)} collective-permute-done((f32[2048,128]{1,0:T(8,128)S(1)}, f32[2048,128]{1,0:T(8,128)S(1)}, u32[]{:S(2)}, u32[]{:S(2)}) %collective-permute-start.1) | collective-permute-done | bytes 1048608 | tf_op jit(solution)/shard_map/ppermute | solution.py:490
  56.5 0.9 shard_map.89
  57.4 1.9 %collective-permute-start.3 = (f32[2048,128]{1,0:T(8,128)S(1)}, f32[2048,128]{1,0:T(8,128)S(1)}, u32[]{:S(2)}, u32[]{:S(2)}) collective-permute-start(f32[2048,128]{1,0:T(8,128)S(1)} %get-tuple-element.41), channel_id=1, source_target_pairs={{0,1},{1,2},{2,3},{3,4},{4,5},{5,6},{6,7},{7,8},{8,9},{9,10},{10,1... | collective-permute-start | bytes 3145736 | tf_op jit(solution)/shard_map/ppermute | solution.py:490
  59.4 10.3 %collective-permute-done.4.refs_0_ = f32[2048,128]{1,0:T(8,128)S(1)} collective-permute-done((f32[2048,128]{1,0:T(8,128)S(1)}, f32[2048,128]{1,0:T(8,128)S(1)}, u32[]{:S(2)}, u32[]{:S(2)}) %collective-permute-start.4) | collective-permute-done | bytes 1048608 | tf_op jit(solution)/shard_map/ppermute | solution.py:490
  69.6 2.0 %shard_map.90 = (f32[2048,128]{1,0:T(8,128)S(1)}, f32[2048,128]{1,0:T(8,128)S(1)}) custom-call(f32[2048,128]{1,0:T(8,128)S(1)} %collective-permute-done.4.refs_0_, f32[2048,128]{1,0:T(8,128)S(1)} %get-tuple-element.40.refs_1_, f32[2048,128]{1,0:T(8,128)S(1)} %get-tuple-element.43.refs_2_, f32[288,128]{1,0:T(8,128)S(1)} %copy-done), custom_call_target="tpu_custom_call" | custom-call | flops 1000 | bytes 1000 | tf_op jit(solution)/shard_map/pallas_call | solution.py:305
  71.6 1.9 %collective-permute-start.12 = (f32[2048,128]{1,0:T(8,128)S(1)}, f32[2048,128]{1,0:T(8,128)S(1)}, u32[]{:S(2)}, u32[]{:S(2)}) collective-permute-start(f32[2048,128]{1,0:T(8,128)S(1)} %get-tuple-element.60), channel_id=1, source_target_pairs={{0,1},{1,2},{2,3},{3,4},{4,5},{5,6},{6,7},{7,8},{8,9},{9,10},{10,1... | collective-permute-start | bytes 3145736 | tf_op jit(solution)/shard_map/ppermute | solution.py:490
  73.7 0.7 collective-permute-start.16
  74.5 1.3 %collective-permute-start.15 = (f32[2056,128]{1,0:T(8,128)S(1)}, f32[2056,128]{1,0:T(8,128)S(1)}, u32[]{:S(2)}, u32[]{:S(2)}) collective-permute-start(f32[2056,128]{1,0:T(8,128)S(1)} %get-tuple-element.58.refs_3_), channel_id=1, source_target_pairs={{32,67},{33,68},{34,69},{35,70},{36,71},{37,72},{38,73},{39,74},{4... | collective-permute-start | bytes 3158024 | tf_op jit(solution)/shard_map/ppermute | solution.py:490
  75.8 9.6 %collective-permute-done.3.refs_0_ = f32[2048,128]{1,0:T(8,128)S(1)} collective-permute-done((f32[2048,128]{1,0:T(8,128)S(1)}, f32[2048,128]{1,0:T(8,128)S(1)}, u32[]{:S(2)}, u32[]{:S(2)}) %collective-permute-start.3) | collective-permute-done | bytes 1048608 | tf_op jit(solution)/shard_map/ppermute | solution.py:490
  85.3 1.8 %shard_map.97 = (f32[2048,128]{1,0:T(8,128)S(1)}, f32[2048,128]{1,0:T(8,128)S(1)}) custom-call(f32[2048,128]{1,0:T(8,128)S(1)} %collective-permute-done.3.refs_0_, f32[2048,128]{1,0:T(8,128)S(1)} %get-tuple-element.44.refs_1_, f32[288,128]{1,0:T(8,128)S(1)} %copy-done, f32[2056,128]{1,0:T(8,128)S(1)} %get-tuple-element.58.refs_3_), custom_call_target="tpu_custom_call" | custom-call | flops 1000 | bytes 1000 | tf_op jit(solution)/shard_map/pallas_call | solution.py:305
  87.1 1.4 %collective-permute-start.11 = (f32[2048,128]{1,0:T(8,128)S(1)}, f32[2048,128]{1,0:T(8,128)S(1)}, u32[]{:S(2)}, u32[]{:S(2)}) collective-permute-start(f32[2048,128]{1,0:T(8,128)S(1)} %get-tuple-element.59), channel_id=1, source_target_pairs={{0,32},{1,33},{2,34},{3,35},{4,36},{5,37},{6,38},{7,39},{8,40},{9,... | collective-permute-start | bytes 3145736 | tf_op jit(solution)/shard_map/ppermute | solution.py:490
  88.5 15.9 %collective-permute-done.12.refs_0_ = f32[2048,128]{1,0:T(8,128)S(1)} collective-permute-done((f32[2048,128]{1,0:T(8,128)S(1)}, f32[2048,128]{1,0:T(8,128)S(1)}, u32[]{:S(2)}, u32[]{:S(2)}) %collective-permute-start.12) | collective-permute-done | bytes 1048608 | tf_op jit(solution)/shard_map/ppermute | solution.py:490
  104.4 3.7 %shard_map.98 = (f32[2048,128]{1,0:T(8,128)S(1)}, f32[2048,128]{1,0:T(8,128)S(1)}) custom-call(f32[2048,128]{1,0:T(8,128)S(1)} %collective-permute-done.12.refs_0_, f32[2048,128]{1,0:T(8,128)S(1)} %get-tuple-element.44.refs_1_, f32[2048,128]{1,0:T(8,128)S(1)} %get-tuple-element.61.refs_2_, f32[288,128]{1,0:T(8,128)S(1)} %copy-done, ...), custom_call_target="tpu_custom_call" | custom-call | flops 1000 | bytes 1000 | tf_op jit(solution)/shard_map/pallas_call | solution.py:305
  108.2 18.2 %collective-permute-done.15.late = f32[2056,128]{1,0:T(8,128)S(1)} collective-permute-done((f32[2056,128]{1,0:T(8,128)S(1)}, f32[2056,128]{1,0:T(8,128)S(1)}, u32[]{:S(2)}, u32[]{:S(2)}) %collective-permute-start.15) | collective-permute-done | bytes 1052704 | tf_op jit(solution)/shard_map/ppermute | solution.py:490
  126.4 2.1 %shard_map.99 = (f32[4096,128]{1,0:T(8,128)}, f32[2048,128]{1,0:T(8,128)}) custom-call(f32[2048,128]{1,0:T(8,128)S(1)} %collective-permute-done.11.first, f32[2048,128]{1,0:T(8,128)S(1)} %collective-permute-done.14.second, f32[2056,128]{1,0:T(8,128)S(1)} %collective-permute-done.15.late, f32[2048,128]{1,0:T(8,128)S(1)} %get-tuple-element.64.stayed, ...), custom_call_target="tpu_custom_call" | custom-call | tf_op jit(solution)/shard_map/pallas_call | solution.py:472
  (22 shorter events, 0.9 us)
Async XLA Ops:
  6.5 7.4 %collective-permute-start.6 = (f32[1312,128]{1,0:T(8,128)}, f32[1312,128]{1,0:T(8,128)S(1)}, u32[]{:S(2)}, u32[]{:S(2)}) collective-permute-start(f32[1312,128]{1,0:T(8,128)} %get-tuple-element.47), channel_id=1, source_target_pairs={{32,63},{33,32},{34,33},{35,34},{36,35},{37,36},{38,37},{39,38},{4... | collective-permute-start | bytes 2015240 | tf_op jit(solution)/shard_map/ppermute | solution.py:490
  7.2 9.1 %collective-permute-start.5 = (f32[1024,128]{1,0:T(8,128)}, f32[1024,128]{1,0:T(8,128)S(1)}, u32[]{:S(2)}, u32[]{:S(2)}) collective-permute-start(f32[1024,128]{1,0:T(8,128)} %get-tuple-element.45), channel_id=1, source_target_pairs={{32,63},{33,32},{34,33},{35,34},{36,35},{37,36},{38,37},{39,38},{4... | collective-permute-start | bytes 1572872 | tf_op jit(solution)/shard_map/ppermute | solution.py:490
  7.9 24.4 %collective-permute-start = (f32[2048,128]{1,0:T(8,128)}, f32[2048,128]{1,0:T(8,128)S(1)}, u32[]{:S(2)}, u32[]{:S(2)}) collective-permute-start(f32[2048,128]{1,0:T(8,128)} %get-tuple-element.34), channel_id=1, source_target_pairs={{0,1},{1,2},{2,3},{3,4},{4,5},{5,6},{6,7},{7,8},{8,9},{9,10},{10,1... | collective-permute-start | bytes 3145736 | tf_op jit(solution)/shard_map/ppermute | solution.py:490
  11.4 32.2 %collective-permute-start.2 = (f32[2048,128]{1,0:T(8,128)}, f32[2048,128]{1,0:T(8,128)S(1)}, u32[]{:S(2)}, u32[]{:S(2)}) collective-permute-start(f32[2048,128]{1,0:T(8,128)} %get-tuple-element.38), channel_id=1, source_target_pairs={{0,1},{1,2},{2,3},{3,4},{4,5},{5,6},{6,7},{7,8},{8,9},{9,10},{10,1... | collective-permute-start | bytes 3145736 | tf_op jit(solution)/shard_map/ppermute | solution.py:490
  13.9 1.6 %copy-start.2 = (f32[4096,128]{1,0:T(8,128)S(1)}, f32[4096,128]{1,0:T(8,128)}, u32[]{:S(2)}) copy-start(f32[4096,128]{1,0:T(8,128)} %get-tuple-element.46.refs_1_) | copy-start | bytes 6291460
  15.6 33.6 %collective-permute-start.8 = (f32[1216,128]{1,0:T(8,128)S(1)}, f32[1216,128]{1,0:T(8,128)S(1)}, u32[]{:S(2)}, u32[]{:S(2)}) collective-permute-start(f32[1216,128]{1,0:T(8,128)S(1)} %get-tuple-element.51), channel_id=1, source_target_pairs={{32,63},{33,32},{34,33},{35,34},{36,35},{37,36},{38,37},{39,38},{4... | collective-permute-start | bytes 1867784 | tf_op jit(solution)/shard_map/ppermute | solution.py:490
  16.3 16.0 %copy-start = (f32[288,128]{1,0:T(8,128)S(1)}, f32[288,128]{1,0:T(8,128)}, u32[]{:S(2)}) copy-start(f32[288,128]{1,0:T(8,128)} %get-tuple-element.36.refs_2_.refs_3_) | copy-start | bytes 442372
  16.3 16.0 %copy-start.1 = (f32[2048,128]{1,0:T(8,128)S(1)}, f32[2048,128]{1,0:T(8,128)}, u32[]{:S(2)}) copy-start(f32[2048,128]{1,0:T(8,128)} %get-tuple-element.35.refs_1_) | copy-start | bytes 3145732
  16.5 33.5 %collective-permute-start.7 = (f32[1024,128]{1,0:T(8,128)S(1)}, f32[1024,128]{1,0:T(8,128)S(1)}, u32[]{:S(2)}, u32[]{:S(2)}) collective-permute-start(f32[1024,128]{1,0:T(8,128)S(1)} %get-tuple-element.49), channel_id=1, source_target_pairs={{32,63},{33,32},{34,33},{35,34},{36,35},{37,36},{38,37},{39,38},{4... | collective-permute-start | bytes 1572872 | tf_op jit(solution)/shard_map/ppermute | solution.py:490
  34.1 22.4 %collective-permute-start.1 = (f32[2048,128]{1,0:T(8,128)S(1)}, f32[2048,128]{1,0:T(8,128)S(1)}, u32[]{:S(2)}, u32[]{:S(2)}) collective-permute-start(f32[2048,128]{1,0:T(8,128)S(1)} %get-tuple-element.37), channel_id=1, source_target_pairs={{0,1},{1,2},{2,3},{3,4},{4,5},{5,6},{6,7},{7,8},{8,9},{9,10},{10,1... | collective-permute-start | bytes 3145736 | tf_op jit(solution)/shard_map/ppermute | solution.py:490
  47.2 22.4 %collective-permute-start.4 = (f32[2048,128]{1,0:T(8,128)S(1)}, f32[2048,128]{1,0:T(8,128)S(1)}, u32[]{:S(2)}, u32[]{:S(2)}) collective-permute-start(f32[2048,128]{1,0:T(8,128)S(1)} %get-tuple-element.42), channel_id=1, source_target_pairs={{0,1},{1,2},{2,3},{3,4},{4,5},{5,6},{6,7},{7,8},{8,9},{9,10},{10,1... | collective-permute-start | bytes 3145736 | tf_op jit(solution)/shard_map/ppermute | solution.py:490
  49.3 1.6 %collective-permute-start.10 = (f32[1120,128]{1,0:T(8,128)S(1)}, f32[1120,128]{1,0:T(8,128)S(1)}, u32[]{:S(2)}, u32[]{:S(2)}) collective-permute-start(f32[1120,128]{1,0:T(8,128)S(1)} %get-tuple-element.55), channel_id=1, source_target_pairs={{32,63},{33,32},{34,33},{35,34},{36,35},{37,36},{38,37},{39,38},{4... | collective-permute-start | bytes 1720328 | tf_op jit(solution)/shard_map/ppermute | solution.py:490
  50.2 23.4 %collective-permute-start.9 = (f32[1024,128]{1,0:T(8,128)S(1)}, f32[1024,128]{1,0:T(8,128)S(1)}, u32[]{:S(2)}, u32[]{:S(2)}) collective-permute-start(f32[1024,128]{1,0:T(8,128)S(1)} %get-tuple-element.53), channel_id=1, source_target_pairs={{32,63},{33,32},{34,33},{35,34},{36,35},{37,36},{38,37},{39,38},{4... | collective-permute-start | bytes 1572872 | tf_op jit(solution)/shard_map/ppermute | solution.py:490
  51.0 37.5 %collective-permute-start.13 = (f32[2048,128]{1,0:T(8,128)S(1)}, f32[2048,128]{1,0:T(8,128)S(1)}, u32[]{:S(2)}, u32[]{:S(2)}) collective-permute-start(f32[2048,128]{1,0:T(8,128)S(1)} %get-tuple-element.62), channel_id=1, source_target_pairs={{32,99},{33,100},{34,101},{35,102},{36,103},{37,104},{38,105},{39,... | collective-permute-start | bytes 3145736 | tf_op jit(solution)/shard_map/ppermute | solution.py:490
  57.4 27.9 %collective-permute-start.3 = (f32[2048,128]{1,0:T(8,128)S(1)}, f32[2048,128]{1,0:T(8,128)S(1)}, u32[]{:S(2)}, u32[]{:S(2)}) collective-permute-start(f32[2048,128]{1,0:T(8,128)S(1)} %get-tuple-element.41), channel_id=1, source_target_pairs={{0,1},{1,2},{2,3},{3,4},{4,5},{5,6},{6,7},{7,8},{8,9},{9,10},{10,1... | collective-permute-start | bytes 3145736 | tf_op jit(solution)/shard_map/ppermute | solution.py:490
  71.6 32.8 %collective-permute-start.12 = (f32[2048,128]{1,0:T(8,128)S(1)}, f32[2048,128]{1,0:T(8,128)S(1)}, u32[]{:S(2)}, u32[]{:S(2)}) collective-permute-start(f32[2048,128]{1,0:T(8,128)S(1)} %get-tuple-element.60), channel_id=1, source_target_pairs={{0,1},{1,2},{2,3},{3,4},{4,5},{5,6},{6,7},{7,8},{8,9},{9,10},{10,1... | collective-permute-start | bytes 3145736 | tf_op jit(solution)/shard_map/ppermute | solution.py:490
  73.7 34.5 %collective-permute-start.16 = (f32[2056,128]{1,0:T(8,128)S(1)}, f32[2056,128]{1,0:T(8,128)S(1)}, u32[]{:S(2)}, u32[]{:S(2)}) collective-permute-start(f32[2056,128]{1,0:T(8,128)S(1)} %get-tuple-element.65), channel_id=1, source_target_pairs={{32,35},{33,36},{34,37},{35,38},{36,39},{37,40},{38,41},{39,42},{4... | collective-permute-start | bytes 3158024 | tf_op jit(solution)/shard_map/ppermute | solution.py:490
  74.5 52.0 %collective-permute-start.15 = (f32[2056,128]{1,0:T(8,128)S(1)}, f32[2056,128]{1,0:T(8,128)S(1)}, u32[]{:S(2)}, u32[]{:S(2)}) collective-permute-start(f32[2056,128]{1,0:T(8,128)S(1)} %get-tuple-element.58.refs_3_), channel_id=1, source_target_pairs={{32,67},{33,68},{34,69},{35,70},{36,71},{37,72},{38,73},{39,74},{4... | collective-permute-start | bytes 3158024 | tf_op jit(solution)/shard_map/ppermute | solution.py:490
  87.1 39.3 %collective-permute-start.11 = (f32[2048,128]{1,0:T(8,128)S(1)}, f32[2048,128]{1,0:T(8,128)S(1)}, u32[]{:S(2)}, u32[]{:S(2)}) collective-permute-start(f32[2048,128]{1,0:T(8,128)S(1)} %get-tuple-element.59), channel_id=1, source_target_pairs={{0,32},{1,33},{2,34},{3,35},{4,36},{5,37},{6,38},{7,39},{8,40},{9,... | collective-permute-start | bytes 3145736 | tf_op jit(solution)/shard_map/ppermute | solution.py:490
  108.1 18.4 %collective-permute-start.14 = (f32[2048,128]{1,0:T(8,128)S(1)}, f32[2048,128]{1,0:T(8,128)S(1)}, u32[]{:S(2)}, u32[]{:S(2)}) collective-permute-start(f32[2048,128]{1,0:T(8,128)S(1)} %get-tuple-element.63), channel_id=1, source_target_pairs={{0,32},{1,33},{2,34},{3,35},{4,36},{5,37},{6,38},{7,39},{8,40},{9,... | collective-permute-start | bytes 3145736 | tf_op jit(solution)/shard_map/ppermute | solution.py:504

commit v4 on v3

--- a/solution.py
+++ b/solution.py
@@ -175,8 +175,16 @@
         dv, dc = slot_update(v_old[tile(vi), :], c_old[tile(ci), :], pos_row, rows, live)
         return v_new, vi, dv, c_new, ci, dc
 
+    odd = group_odd()
+    kept = pltpu.make_async_copy(own, own_out, sems.at[5])
+    sent = pltpu.make_async_copy(
+        own, moved_out.at[pl.ds(QUARTER, LISTED * (steps - 1))], sems.at[6]
+    )
+    kept.start()
+    sent.start()
     run_pairs(chosen, mine, one)
-    odd = group_odd()
+    kept.wait()
+    sent.wait()
 
     @pl.when(odd == 0)
     def even_group():
@@ -184,7 +192,6 @@
             (v_new.at[pl.ds(0, HALF)], low_out),
             (v_new.at[pl.ds(HALF, HALF)], high_out),
             (c_new, ctx_out),
-            (own, own_out),
         ]
         waited(moved(stores, sems))
 
@@ -192,7 +199,6 @@
     def odd_group():
         stores = [
             (c_new.at[pl.ds(0, QUARTER)], moved_out.at[pl.ds(0, QUARTER)]),
-            (own, moved_out.at[pl.ds(QUARTER, LISTED * (steps - 1))]),
             (c_new.at[pl.ds(QUARTER, QUARTER)], moved_high),
             (v_new, vert_out),
         ]
@@ -318,7 +324,7 @@
             pltpu.SemaphoreType.DMA((6,)),
         ],
         compiler_params=pltpu.CompilerParams(vmem_limit_bytes=STEP_LIMIT),
-        cost_estimate=pl.CostEstimate(flops=1000, bytes_accessed=1000, transcendentals=0),
+        cost_estimate=pl.CostEstimate(flops=4000000000, bytes_accessed=1000, transcendentals=0),
     )(*operands)
 
 
@@ -438,7 +444,7 @@
             pltpu.SemaphoreType.DMA((13,)),
         ],
         compiler_params=pltpu.CompilerParams(vmem_limit_bytes=STEP_LIMIT),
-        cost_estimate=pl.CostEstimate(flops=16000000000, bytes_accessed=1000, transcendentals=0),
+        cost_estimate=pl.CostEstimate(flops=2000000000, bytes_accessed=1000, transcendentals=0),
     )(*operands, *after)
 
 

time: 128 us -> 129 us (level)
  waiting for transfers between devices: 81.3 us -> 82.8 us
    pallas_call x6, Pallas kernels: 13.9 us -> 12 us  [even_step(): pl.pallas_call(kernel, out_shape=[wide(size), wide(HALF)], in_specs=[ANY]...]
    pallas_call x1, Pallas kernels: 5.83 us -> 7.65 us  [first_step(): pl.pallas_call(kernel, out_shape=[wide(HALF), wide(HALF), wide(QUARTER +...]
    ppermute x16, waiting for transfers between devices: 81.2 us -> 82.8 us  [sent(): return lax.ppermute(array, AXES, route(groups, members, odd, move))]
  transfers between devices with their start and end apart: 17 -> 17, of which waited for: 7 -> 7; matrix products, arithmetic and copies ran while one was open for 0% -> 0% of each run, Pallas kernels for 11% -> 10%
where the time goes in v4:
time: 129 us
  waiting for transfers between devices  82.8 us (64%)
  Pallas kernels  22.5 us (17%)
  starting transfers between devices  21.2 us (16%)
  local copies, waits for them, and re-layouts  1.59 us (1%)
    ppermute x16, waiting for transfers between devices, sent(): return lax.ppermute(array, AXES, route(groups, members, odd, move))  82.8 us
    ppermute x16, starting transfers between devices, sent(): return lax.ppermute(array, AXES, route(groups, members, odd, move))  21.1 us
    pallas_call x6, Pallas kernels, even_step(): pl.pallas_call(kernel, out_shape=[wide(size), wide(HALF)], in_specs=[ANY]...  12 us
    pallas_call x1, Pallas kernels, first_step(): pl.pallas_call(kernel, out_shape=[wide(HALF), wide(HALF), wide(QUARTER +...  7.65 us
  transfers between devices with their start and end apart: 17, of which 7 were waited for; matrix products, arithmetic and copies ran while one was open for 0% of the time, Pallas kernels for 10%

profile of v4, /device:TPU:0, one launch (start us, length us, event | category | flops | bytes accessed | tf_op | source)
XLA Modules:
  0.0 129.3 jit_solution(3450217067210902888)
XLA Ops:
  0.6 7.7 %shard_map.86 = (f32[2048,128]{1,0:T(8,128)}, f32[2048,128]{1,0:T(8,128)}, f32[1312,128]{1,0:T(8,128)}, f32[1024,128]{1,0:T(8,128)}, f32[2048,128]{1,0:T(8,128)}...) custom-call(f32[4096,128]{1,0:T(8,128)} %refs_0_.1, f32[2048,128]{1,0:T(8,128)} %refs_1_.1, s32[4]{0:T(128)} %refs_2_.1, ...), custom_call_target="tpu_custom_call" | custom-call | flops 1000 | bytes 1000 | tf_op jit(solution)/shard_map/pallas_call | solution.py:215
  8.3 0.7 collective-permute-start.6
  9.0 1.9 %collective-permute-start = (f32[2048,128]{1,0:T(8,128)}, f32[2048,128]{1,0:T(8,128)S(1)}, u32[]{:S(2)}, u32[]{:S(2)}) collective-permute-start(f32[2048,128]{1,0:T(8,128)} %get-tuple-element.34), channel_id=1, source_target_pairs={{0,1},{1,2},{2,3},{3,4},{4,5},{5,6},{6,7},{7,8},{8,9},{9,10},{10,1... | collective-permute-start | bytes 3145736 | tf_op jit(solution)/shard_map/ppermute | solution.py:496
  10.9 0.7 collective-permute-start.5
  11.6 3.1 %collective-permute-start.2 = (f32[2048,128]{1,0:T(8,128)}, f32[2048,128]{1,0:T(8,128)S(1)}, u32[]{:S(2)}, u32[]{:S(2)}) collective-permute-start(f32[2048,128]{1,0:T(8,128)} %get-tuple-element.38), channel_id=1, source_target_pairs={{0,1},{1,2},{2,3},{3,4},{4,5},{5,6},{6,7},{7,8},{8,9},{9,10},{10,1... | collective-permute-start | bytes 3145736 | tf_op jit(solution)/shard_map/ppermute | solution.py:496
  14.8 1.6 %copy-done = f32[4096,128]{1,0:T(8,128)S(1)} copy-done((f32[4096,128]{1,0:T(8,128)S(1)}, f32[4096,128]{1,0:T(8,128)}, u32[]{:S(2)}) %copy-start) | copy-done | bytes 2097176
  16.5 0.7 collective-permute-start.8
  17.4 0.8 collective-permute-start.7
  18.2 13.4 %collective-permute-done.refs_0_ = f32[2048,128]{1,0:T(8,128)S(1)} collective-permute-done((f32[2048,128]{1,0:T(8,128)}, f32[2048,128]{1,0:T(8,128)S(1)}, u32[]{:S(2)}, u32[]{:S(2)}) %collective-permute-start) | collective-permute-done | bytes 1048608 | tf_op jit(solution)/shard_map/ppermute | solution.py:496
  31.6 1.8 %shard_map.87 = (f32[2048,128]{1,0:T(8,128)S(1)}, f32[2048,128]{1,0:T(8,128)S(1)}) custom-call(f32[2048,128]{1,0:T(8,128)S(1)} %collective-permute-done.refs_0_, f32[2048,128]{1,0:T(8,128)S(1)} %copy-done.1, f32[288,128]{1,0:T(8,128)S(1)} %copy-done.2), custom_call_target="tpu_custom_call" | custom-call | flops 4000000000 | bytes 1000 | tf_op jit(solution)/shard_map/pallas_call | solution.py:311
  33.5 1.9 %collective-permute-start.1 = (f32[2048,128]{1,0:T(8,128)S(1)}, f32[2048,128]{1,0:T(8,128)S(1)}, u32[]{:S(2)}, u32[]{:S(2)}) collective-permute-start(f32[2048,128]{1,0:T(8,128)S(1)} %get-tuple-element.37), channel_id=1, source_target_pairs={{0,1},{1,2},{2,3},{3,4},{4,5},{5,6},{6,7},{7,8},{8,9},{9,10},{10,1... | collective-permute-start | bytes 3145736 | tf_op jit(solution)/shard_map/ppermute | solution.py:496
  35.5 0.7 collective-permute-start.10
  36.2 6.6 %collective-permute-done.2.refs_0_ = f32[2048,128]{1,0:T(8,128)S(1)} collective-permute-done((f32[2048,128]{1,0:T(8,128)}, f32[2048,128]{1,0:T(8,128)S(1)}, u32[]{:S(2)}, u32[]{:S(2)}) %collective-permute-start.2) | collective-permute-done | bytes 1048608 | tf_op jit(solution)/shard_map/ppermute | solution.py:496
  42.9 2.7 %shard_map.88 = (f32[2048,128]{1,0:T(8,128)S(1)}, f32[2048,128]{1,0:T(8,128)S(1)}) custom-call(f32[2048,128]{1,0:T(8,128)S(1)} %collective-permute-done.2.refs_0_, f32[2048,128]{1,0:T(8,128)S(1)} %copy-done.1, f32[2048,128]{1,0:T(8,128)S(1)} %get-tuple-element.39.refs_2_, f32[288,128]{1,0:T(8,128)S(1)} %copy-done.2), custom_call_target="tpu_custom_call" | custom-call | flops 4000000000 | bytes 1000 | tf_op jit(solution)/shard_map/pallas_call | solution.py:311
  45.6 1.9 %collective-permute-start.4 = (f32[2048,128]{1,0:T(8,128)S(1)}, f32[2048,128]{1,0:T(8,128)S(1)}, u32[]{:S(2)}, u32[]{:S(2)}) collective-permute-start(f32[2048,128]{1,0:T(8,128)S(1)} %get-tuple-element.42), channel_id=1, source_target_pairs={{0,1},{1,2},{2,3},{3,4},{4,5},{5,6},{6,7},{7,8},{8,9},{9,10},{10,1... | collective-permute-start | bytes 3145736 | tf_op jit(solution)/shard_map/ppermute | solution.py:496
  47.7 0.7 collective-permute-start.9
  48.6 7.3 %collective-permute-done.1.refs_0_ = f32[2048,128]{1,0:T(8,128)S(1)} collective-permute-done((f32[2048,128]{1,0:T(8,128)S(1)}, f32[2048,128]{1,0:T(8,128)S(1)}, u32[]{:S(2)}, u32[]{:S(2)}) %collective-permute-start.1) | collective-permute-done | bytes 1048608 | tf_op jit(solution)/shard_map/ppermute | solution.py:496
  55.9 1.8 %shard_map.89 = (f32[2048,128]{1,0:T(8,128)S(1)}, f32[2048,128]{1,0:T(8,128)S(1)}) custom-call(f32[2048,128]{1,0:T(8,128)S(1)} %collective-permute-done.1.refs_0_, f32[2048,128]{1,0:T(8,128)S(1)} %get-tuple-element.40.refs_1_, f32[288,128]{1,0:T(8,128)S(1)} %copy-done.2), custom_call_target="tpu_custom_call" | custom-call | flops 4000000000 | bytes 1000 | tf_op jit(solution)/shard_map/pallas_call | solution.py:311
  57.7 1.9 %collective-permute-start.3 = (f32[2048,128]{1,0:T(8,128)S(1)}, f32[2048,128]{1,0:T(8,128)S(1)}, u32[]{:S(2)}, u32[]{:S(2)}) collective-permute-start(f32[2048,128]{1,0:T(8,128)S(1)} %get-tuple-element.41), channel_id=1, source_target_pairs={{0,1},{1,2},{2,3},{3,4},{4,5},{5,6},{6,7},{7,8},{8,9},{9,10},{10,1... | collective-permute-start | bytes 3145736 | tf_op jit(solution)/shard_map/ppermute | solution.py:496
  59.6 0.7 collective-permute-start.13
  60.4 7.7 %collective-permute-done.4.refs_0_ = f32[2048,128]{1,0:T(8,128)S(1)} collective-permute-done((f32[2048,128]{1,0:T(8,128)S(1)}, f32[2048,128]{1,0:T(8,128)S(1)}, u32[]{:S(2)}, u32[]{:S(2)}) %collective-permute-start.4) | collective-permute-done | bytes 1048608 | tf_op jit(solution)/shard_map/ppermute | solution.py:496
  68.0 2.0 %shard_map.90 = (f32[2048,128]{1,0:T(8,128)S(1)}, f32[2048,128]{1,0:T(8,128)S(1)}) custom-call(f32[2048,128]{1,0:T(8,128)S(1)} %collective-permute-done.4.refs_0_, f32[2048,128]{1,0:T(8,128)S(1)} %get-tuple-element.40.refs_1_, f32[2048,128]{1,0:T(8,128)S(1)} %get-tuple-element.43.refs_2_, f32[288,128]{1,0:T(8,128)S(1)} %copy-done.2), custom_call_target="tpu_custom_call" | custom-call | flops 4000000000 | bytes 1000 | tf_op jit(solution)/shard_map/pallas_call | solution.py:311
  70.0 1.9 %collective-permute-start.12 = (f32[2048,128]{1,0:T(8,128)S(1)}, f32[2048,128]{1,0:T(8,128)S(1)}, u32[]{:S(2)}, u32[]{:S(2)}) collective-permute-start(f32[2048,128]{1,0:T(8,128)S(1)} %get-tuple-element.60), channel_id=1, source_target_pairs={{0,1},{1,2},{2,3},{3,4},{4,5},{5,6},{6,7},{7,8},{8,9},{9,10},{10,1... | collective-permute-start | bytes 3145736 | tf_op jit(solution)/shard_map/ppermute | solution.py:496
  72.1 0.7 collective-permute-start.16
  72.9 1.3 collective-permute-start.15
  74.2 9.8 %collective-permute-done.3.refs_0_ = f32[2048,128]{1,0:T(8,128)S(1)} collective-permute-done((f32[2048,128]{1,0:T(8,128)S(1)}, f32[2048,128]{1,0:T(8,128)S(1)}, u32[]{:S(2)}, u32[]{:S(2)}) %collective-permute-start.3) | collective-permute-done | bytes 1048608 | tf_op jit(solution)/shard_map/ppermute | solution.py:496
  84.0 1.8 %shard_map.97 = (f32[2048,128]{1,0:T(8,128)S(1)}, f32[2048,128]{1,0:T(8,128)S(1)}) custom-call(f32[2048,128]{1,0:T(8,128)S(1)} %collective-permute-done.3.refs_0_, f32[2048,128]{1,0:T(8,128)S(1)} %get-tuple-element.44.refs_1_, f32[288,128]{1,0:T(8,128)S(1)} %copy-done.2, f32[2056,128]{1,0:T(8,128)S(1)} %get-tuple-element.58.refs_3_), custom_call_target="tpu_custom_call" | custom-call | flops 4000000000 | bytes 1000 | tf_op jit(solution)/shard_map/pallas_call | solution.py:311
  85.8 1.4 %collective-permute-start.11 = (f32[2048,128]{1,0:T(8,128)S(1)}, f32[2048,128]{1,0:T(8,128)S(1)}, u32[]{:S(2)}, u32[]{:S(2)}) collective-permute-start(f32[2048,128]{1,0:T(8,128)S(1)} %get-tuple-element.59), channel_id=1, source_target_pairs={{0,32},{1,33},{2,34},{3,35},{4,36},{5,37},{6,38},{7,39},{8,40},{9,... | collective-permute-start | bytes 3145736 | tf_op jit(solution)/shard_map/ppermute | solution.py:496
  87.2 15.4 %collective-permute-done.12.refs_0_ = f32[2048,128]{1,0:T(8,128)S(1)} collective-permute-done((f32[2048,128]{1,0:T(8,128)S(1)}, f32[2048,128]{1,0:T(8,128)S(1)}, u32[]{:S(2)}, u32[]{:S(2)}) %collective-permute-start.12) | collective-permute-done | bytes 1048608 | tf_op jit(solution)/shard_map/ppermute | solution.py:496
  102.6 1.8 %shard_map.98 = (f32[2048,128]{1,0:T(8,128)S(1)}, f32[2048,128]{1,0:T(8,128)S(1)}) custom-call(f32[2048,128]{1,0:T(8,128)S(1)} %collective-permute-done.12.refs_0_, f32[2048,128]{1,0:T(8,128)S(1)} %get-tuple-element.44.refs_1_, f32[2048,128]{1,0:T(8,128)S(1)} %get-tuple-element.61.refs_2_, f32[288,128]{1,0:T(8,128)S(1)} %copy-done.2, ...), custom_call_target="tpu_custom_call" | custom-call | flops 4000000000 | bytes 1000 | tf_op jit(solution)/shard_map/pallas_call | solution.py:311
  104.5 22.5 %collective-permute-done.15.late = f32[2056,128]{1,0:T(8,128)S(1)} collective-permute-done((f32[2056,128]{1,0:T(8,128)S(1)}, f32[2056,128]{1,0:T(8,128)S(1)}, u32[]{:S(2)}, u32[]{:S(2)}) %collective-permute-start.15) | collective-permute-done | bytes 1052704 | tf_op jit(solution)/shard_map/ppermute | solution.py:496
  127.0 2.1 %shard_map.99 = (f32[4096,128]{1,0:T(8,128)}, f32[2048,128]{1,0:T(8,128)}) custom-call(f32[2048,128]{1,0:T(8,128)S(1)} %collective-permute-done.11.first, f32[2048,128]{1,0:T(8,128)S(1)} %collective-permute-done.14.second, f32[2056,128]{1,0:T(8,128)S(1)} %collective-permute-done.15.late, f32[2048,128]{1,0:T(8,128)S(1)} %get-tuple-element.64.stayed, ...), custom_call_target="tpu_custom_call" | custom-call | tf_op jit(solution)/shard_map/pallas_call | solution.py:478
  (22 shorter events, 0.9 us)
Async XLA Ops:
  8.3 6.5 %collective-permute-start.6 = (f32[1312,128]{1,0:T(8,128)}, f32[1312,128]{1,0:T(8,128)S(1)}, u32[]{:S(2)}, u32[]{:S(2)}) collective-permute-start(f32[1312,128]{1,0:T(8,128)} %get-tuple-element.47), channel_id=1, source_target_pairs={{32,63},{33,32},{34,33},{35,34},{36,35},{37,36},{38,37},{39,38},{4... | collective-permute-start | bytes 2015240 | tf_op jit(solution)/shard_map/ppermute | solution.py:496
  9.0 22.6 %collective-permute-start = (f32[2048,128]{1,0:T(8,128)}, f32[2048,128]{1,0:T(8,128)S(1)}, u32[]{:S(2)}, u32[]{:S(2)}) collective-permute-start(f32[2048,128]{1,0:T(8,128)} %get-tuple-element.34), channel_id=1, source_target_pairs={{0,1},{1,2},{2,3},{3,4},{4,5},{5,6},{6,7},{7,8},{8,9},{9,10},{10,1... | collective-permute-start | bytes 3145736 | tf_op jit(solution)/shard_map/ppermute | solution.py:496
  10.9 6.3 %collective-permute-start.5 = (f32[1024,128]{1,0:T(8,128)}, f32[1024,128]{1,0:T(8,128)S(1)}, u32[]{:S(2)}, u32[]{:S(2)}) collective-permute-start(f32[1024,128]{1,0:T(8,128)} %get-tuple-element.45), channel_id=1, source_target_pairs={{32,63},{33,32},{34,33},{35,34},{36,35},{37,36},{38,37},{39,38},{4... | collective-permute-start | bytes 1572872 | tf_op jit(solution)/shard_map/ppermute | solution.py:496
  11.6 31.2 %collective-permute-start.2 = (f32[2048,128]{1,0:T(8,128)}, f32[2048,128]{1,0:T(8,128)S(1)}, u32[]{:S(2)}, u32[]{:S(2)}) collective-permute-start(f32[2048,128]{1,0:T(8,128)} %get-tuple-element.38), channel_id=1, source_target_pairs={{0,1},{1,2},{2,3},{3,4},{4,5},{5,6},{6,7},{7,8},{8,9},{9,10},{10,1... | collective-permute-start | bytes 3145736 | tf_op jit(solution)/shard_map/ppermute | solution.py:496
  14.8 1.6 %copy-start = (f32[4096,128]{1,0:T(8,128)S(1)}, f32[4096,128]{1,0:T(8,128)}, u32[]{:S(2)}) copy-start(f32[4096,128]{1,0:T(8,128)} %get-tuple-element.46.refs_1_) | copy-start | bytes 6291460
  16.5 18.9 %collective-permute-start.8 = (f32[1216,128]{1,0:T(8,128)S(1)}, f32[1216,128]{1,0:T(8,128)S(1)}, u32[]{:S(2)}, u32[]{:S(2)}) collective-permute-start(f32[1216,128]{1,0:T(8,128)S(1)} %get-tuple-element.51), channel_id=1, source_target_pairs={{32,63},{33,32},{34,33},{35,34},{36,35},{37,36},{38,37},{39,38},{4... | collective-permute-start | bytes 1867784 | tf_op jit(solution)/shard_map/ppermute | solution.py:496
  17.2 14.4 %copy-start.1 = (f32[2048,128]{1,0:T(8,128)S(1)}, f32[2048,128]{1,0:T(8,128)}, u32[]{:S(2)}) copy-start(f32[2048,128]{1,0:T(8,128)} %get-tuple-element.35.refs_1_) | copy-start | bytes 3145732
  17.2 14.4 %copy-start.2 = (f32[288,128]{1,0:T(8,128)S(1)}, f32[288,128]{1,0:T(8,128)}, u32[]{:S(2)}) copy-start(f32[288,128]{1,0:T(8,128)} %get-tuple-element.36.refs_2_.refs_3_) | copy-start | bytes 442372
  17.4 30.2 %collective-permute-start.7 = (f32[1024,128]{1,0:T(8,128)S(1)}, f32[1024,128]{1,0:T(8,128)S(1)}, u32[]{:S(2)}, u32[]{:S(2)}) collective-permute-start(f32[1024,128]{1,0:T(8,128)S(1)} %get-tuple-element.49), channel_id=1, source_target_pairs={{32,63},{33,32},{34,33},{35,34},{36,35},{37,36},{38,37},{39,38},{4... | collective-permute-start | bytes 1572872 | tf_op jit(solution)/shard_map/ppermute | solution.py:496
  33.5 22.4 %collective-permute-start.1 = (f32[2048,128]{1,0:T(8,128)S(1)}, f32[2048,128]{1,0:T(8,128)S(1)}, u32[]{:S(2)}, u32[]{:S(2)}) collective-permute-start(f32[2048,128]{1,0:T(8,128)S(1)} %get-tuple-element.37), channel_id=1, source_target_pairs={{0,1},{1,2},{2,3},{3,4},{4,5},{5,6},{6,7},{7,8},{8,9},{9,10},{10,1... | collective-permute-start | bytes 3145736 | tf_op jit(solution)/shard_map/ppermute | solution.py:496
  35.5 12.9 %collective-permute-start.10 = (f32[1120,128]{1,0:T(8,128)S(1)}, f32[1120,128]{1,0:T(8,128)S(1)}, u32[]{:S(2)}, u32[]{:S(2)}) collective-permute-start(f32[1120,128]{1,0:T(8,128)S(1)} %get-tuple-element.55), channel_id=1, source_target_pairs={{32,63},{33,32},{34,33},{35,34},{36,35},{37,36},{38,37},{39,38},{4... | collective-permute-start | bytes 1720328 | tf_op jit(solution)/shard_map/ppermute | solution.py:496
  45.6 22.4 %collective-permute-start.4 = (f32[2048,128]{1,0:T(8,128)S(1)}, f32[2048,128]{1,0:T(8,128)S(1)}, u32[]{:S(2)}, u32[]{:S(2)}) collective-permute-start(f32[2048,128]{1,0:T(8,128)S(1)} %get-tuple-element.42), channel_id=1, source_target_pairs={{0,1},{1,2},{2,3},{3,4},{4,5},{5,6},{6,7},{7,8},{8,9},{9,10},{10,1... | collective-permute-start | bytes 3145736 | tf_op jit(solution)/shard_map/ppermute | solution.py:496
  47.7 24.3 %collective-permute-start.9 = (f32[1024,128]{1,0:T(8,128)S(1)}, f32[1024,128]{1,0:T(8,128)S(1)}, u32[]{:S(2)}, u32[]{:S(2)}) collective-permute-start(f32[1024,128]{1,0:T(8,128)S(1)} %get-tuple-element.53), channel_id=1, source_target_pairs={{32,63},{33,32},{34,33},{35,34},{36,35},{37,36},{38,37},{39,38},{4... | collective-permute-start | bytes 1572872 | tf_op jit(solution)/shard_map/ppermute | solution.py:496
  57.7 26.3 %collective-permute-start.3 = (f32[2048,128]{1,0:T(8,128)S(1)}, f32[2048,128]{1,0:T(8,128)S(1)}, u32[]{:S(2)}, u32[]{:S(2)}) collective-permute-start(f32[2048,128]{1,0:T(8,128)S(1)} %get-tuple-element.41), channel_id=1, source_target_pairs={{0,1},{1,2},{2,3},{3,4},{4,5},{5,6},{6,7},{7,8},{8,9},{9,10},{10,1... | collective-permute-start | bytes 3145736 | tf_op jit(solution)/shard_map/ppermute | solution.py:496
  59.6 27.5 %collective-permute-start.13 = (f32[2048,128]{1,0:T(8,128)S(1)}, f32[2048,128]{1,0:T(8,128)S(1)}, u32[]{:S(2)}, u32[]{:S(2)}) collective-permute-start(f32[2048,128]{1,0:T(8,128)S(1)} %get-tuple-element.62), channel_id=1, source_target_pairs={{32,99},{33,100},{34,101},{35,102},{36,103},{37,104},{38,105},{39,... | collective-permute-start | bytes 3145736 | tf_op jit(solution)/shard_map/ppermute | solution.py:496
  70.0 32.5 %collective-permute-start.12 = (f32[2048,128]{1,0:T(8,128)S(1)}, f32[2048,128]{1,0:T(8,128)S(1)}, u32[]{:S(2)}, u32[]{:S(2)}) collective-permute-start(f32[2048,128]{1,0:T(8,128)S(1)} %get-tuple-element.60), channel_id=1, source_target_pairs={{0,1},{1,2},{2,3},{3,4},{4,5},{5,6},{6,7},{7,8},{8,9},{9,10},{10,1... | collective-permute-start | bytes 3145736 | tf_op jit(solution)/shard_map/ppermute | solution.py:496
  72.1 32.4 %collective-permute-start.16 = (f32[2056,128]{1,0:T(8,128)S(1)}, f32[2056,128]{1,0:T(8,128)S(1)}, u32[]{:S(2)}, u32[]{:S(2)}) collective-permute-start(f32[2056,128]{1,0:T(8,128)S(1)} %get-tuple-element.65), channel_id=1, source_target_pairs={{32,35},{33,36},{34,37},{35,38},{36,39},{37,40},{38,41},{39,42},{4... | collective-permute-start | bytes 3158024 | tf_op jit(solution)/shard_map/ppermute | solution.py:496
  72.9 54.2 %collective-permute-start.15 = (f32[2056,128]{1,0:T(8,128)S(1)}, f32[2056,128]{1,0:T(8,128)S(1)}, u32[]{:S(2)}, u32[]{:S(2)}) collective-permute-start(f32[2056,128]{1,0:T(8,128)S(1)} %get-tuple-element.58.refs_3_), channel_id=1, source_target_pairs={{32,67},{33,68},{34,69},{35,70},{36,71},{37,72},{38,73},{39,74},{4... | collective-permute-start | bytes 3158024 | tf_op jit(solution)/shard_map/ppermute | solution.py:496
  85.8 41.3 %collective-permute-start.11 = (f32[2048,128]{1,0:T(8,128)S(1)}, f32[2048,128]{1,0:T(8,128)S(1)}, u32[]{:S(2)}, u32[]{:S(2)}) collective-permute-start(f32[2048,128]{1,0:T(8,128)S(1)} %get-tuple-element.59), channel_id=1, source_target_pairs={{0,32},{1,33},{2,34},{3,35},{4,36},{5,37},{6,38},{7,39},{8,40},{9,... | collective-permute-start | bytes 3145736 | tf_op jit(solution)/shard_map/ppermute | solution.py:496
  104.4 22.6 %collective-permute-start.14 = (f32[2048,128]{1,0:T(8,128)S(1)}, f32[2048,128]{1,0:T(8,128)S(1)}, u32[]{:S(2)}, u32[]{:S(2)}) collective-permute-start(f32[2048,128]{1,0:T(8,128)S(1)} %get-tuple-element.63), channel_id=1, source_target_pairs={{0,32},{1,33},{2,34},{3,35},{4,36},{5,37},{6,38},{7,39},{8,40},{9,... | collective-permute-start | bytes 3145736 | tf_op jit(solution)/shard_map/ppermute | solution.py:510
